TPU v7x, 256 devices: a whole 4x4x8 slice. The times are simulated.
256 devices in a mesh: row: 16 (over z, core), col: 16 (over x, y).
Axes of the slice: x: 4, y: 4, z: 8, core: 2. Of those that a mesh axis runs over, the one named last changes fastest.
Arguments:
- context: bfloat16 [4096, 6144], P('row', 'col'), may hold values from -6 to 6
- residual_in: bfloat16 [4096, 6144], P('col', 'row'), may hold values from -70 to 70
- proj_weight: bfloat16 [6144, 6144], P('col', 'row'), may hold values from -0.078125 to 0.078125
- proj_bias: bfloat16 [6144], P('row'), may hold values from -3 to 3
- norm_gain: bfloat16 [6144], P('row'), may hold values from 0.099609375 to 1.8984375
- norm_shift: bfloat16 [6144], P('row'), may hold values from -3 to 3
- up_weight: bfloat16 [6144, 12288], P('row', 'col'), may hold values from -0.078125 to 0.078125
- up_bias: bfloat16 [12288], P('col'), may hold values from -3 to 3
- down_weight: bfloat16 [12288, 6144], P('col', 'row'), may hold values from -0.0546875 to 0.0546875
- down_bias: bfloat16 [6144], P('row'), may hold values from -3 to 3
Outputs:
- layer_out: bfloat16 [4096, 6144], P('col', 'row')
All inputs are finite; a program needn't handle non-finite values.
Results may differ from a plain program's by a relative error of at most 0.015.
Values may be sent and summed in bfloat16 or wider, within the bound.
A program may use at most 64 MiB of HBM per device.

v0:
```python
import jax
import jax.numpy as jnp
from jax import lax
from jax.sharding import PartitionSpec as P

D = 6144


def local(
    context,
    residual_in,
    proj_weight,
    proj_bias,
    norm_gain,
    norm_shift,
    up_weight,
    up_bias,
    down_weight,
    down_bias,
):
    context_all = lax.all_gather(context, "row", axis=0, tiled=True)
    rows_part = context_all
    attended = lax.psum_scatter(
        jnp.dot(rows_part, proj_weight, preferred_element_type=jnp.float32).astype(jnp.bfloat16),
        "col",
        scatter_dimension=0,
        tiled=True,
    ).astype(jnp.float32)
    mixed = residual_in.astype(jnp.float32) + attended + proj_bias.astype(jnp.float32)
    total_sum, total_square = lax.psum(
        (jnp.sum(mixed, axis=1, keepdims=True), jnp.sum(mixed * mixed, axis=1, keepdims=True)),
        "row",
    )
    mean = total_sum / D
    var = total_square / D - mean * mean
    normed = (
        (mixed - mean) * lax.rsqrt(var + 1e-05) * norm_gain.astype(jnp.float32)
        + norm_shift.astype(jnp.float32)
    ).astype(jnp.bfloat16)
    normed_all = lax.all_gather(normed, "col", axis=0, tiled=True)
    rows_part = normed_all
    pre_local = lax.psum_scatter(
        jnp.dot(rows_part, up_weight, preferred_element_type=jnp.float32).astype(jnp.bfloat16),
        "row",
        scatter_dimension=0,
        tiled=True,
    ).astype(jnp.float32)
    hidden_local = jax.nn.gelu(pre_local + up_bias.astype(jnp.float32), approximate=True).astype(
        jnp.bfloat16
    )
    hidden_all = lax.all_gather(hidden_local, "row", axis=0, tiled=True)
    rows_part = hidden_all
    projected = lax.psum_scatter(
        jnp.dot(rows_part, down_weight, preferred_element_type=jnp.float32).astype(jnp.bfloat16),
        "col",
        scatter_dimension=0,
        tiled=True,
    ).astype(jnp.float32)
    return (mixed + projected + down_bias.astype(jnp.float32)).astype(jnp.bfloat16)


def solution(mesh):
    return jax.shard_map(
        local,
        mesh=mesh,
        in_specs=(
            P("row", "col"),
            P("col", "row"),
            P("col", "row"),
            P("row"),
            P("row"),
            P("row"),
            P("row", "col"),
            P("col"),
            P("col", "row"),
            P("row"),
        ),
        out_specs=P("col", "row"),
        check_vma=False,
    )
```

profile of v0, /device:TPU:1, one launch (start us, length us, event | category | flops | bytes accessed | tf_op | source)
XLA Modules:
  0.0 433.2 jit_solution(5471536894944342194)
XLA Ops:
  6.5 0.0 copy-start
  6.5 0.0 all-gather.4.cloned.1.call-start
  6.5 0.7 all-gather.4.cloned.1.call-update
  7.3 0.0 reduce-scatter.4.cloned.1.call-start
  7.3 47.1 %all-gather.4.cloned.1.call-done = bf16[4096,384]{1,0:T(8,128)(2,1)} async-done(((bf16[256,384]{1,0:T(8,128)(2,1)}), bf16[4096,384]{1,0:T(8,128)(2,1)}) %all-gather.4.cloned.1.call-update) | async-done | bytes 3145744 | tf_op jit(solution)/shard_map/all_gather | solution.py:21
  54.4 5.6 %convolution_convert_fusion.1 = bf16[4096,384]{1,0:T(8,128)(2,1)} fusion(bf16[4096,384]{1,0:T(8,128)(2,1)} %all-gather.4.cloned.1.call-done, bf16[384,384]{1,0:T(8,128)(2,1)} %param.12), kind=kOutput, calls=%fused_computation.1 | convolution fusion | flops 1209532416 | bytes 6586368 | tf_op jit(solution)/shard_map/dot_general | solution.py:24
  60.0 0.0 reduce-scatter.4.cloned.1.call-update
  60.0 0.0 all-gather.6.cloned.1.call-start
  60.1 0.6 copy-done.4
  60.7 0.0 copy-done.5
  60.7 0.0 copy-done.6
  60.7 76.8 %reduce-scatter.4.cloned.1.call-done = bf16[256,384]{1,0:T(8,128)(2,1)} async-done(((bf16[4096,384]{1,0:T(8,128)(2,1)}), bf16[256,384]{1,0:T(8,128)(2,1)}) %reduce-scatter.4.cloned.1.call-update) | async-done | bytes 196624 | tf_op jit(solution)/shard_map/reduce_scatter | solution.py:23
  137.6 1.1 fusion.8
  138.7 25.7 %all-reduce = (f32[256,1]{0,1:T(1,128)S(1)}, f32[256,1]{0,1:T(1,128)S(1)}) all-reduce(f32[256,1]{0,1:T(1,128)S(1)} %bitcast.11, f32[256,1]{0,1:T(1,128)S(1)} %bitcast.10), channel_id=1, replica_groups=mesh['row'=16,'col'=16] {'row'}, use_global_device_ids=true, to_apply=%region_4.0 | all-reduce | flops 512 | bytes 4096 | tf_op jit(solution)/shard_map/psum | solution.py:30
  164.4 1.8 add_convert_fusion.1
  166.2 0.0 all-gather.6.cloned.1.call-update
  166.2 0.0 reduce-scatter.6.cloned.1.call-start
  166.2 51.6 %all-gather.6.cloned.1.call-done = bf16[4096,384]{1,0:T(8,128)(2,1)} async-done(((bf16[256,384]{1,0:T(8,128)(2,1)}), bf16[4096,384]{1,0:T(8,128)(2,1)}) %all-gather.6.cloned.1.call-update) | async-done | bytes 3145744 | tf_op jit(solution)/shard_map/all_gather | solution.py:40
  217.8 8.0 %convolution_convert_fusion = bf16[4096,768]{1,0:T(8,128)(2,1)} fusion(bf16[4096,384]{1,0:T(8,128)(2,1)} %all-gather.6.cloned.1.call-done, bf16[384,768]{1,0:T(8,128)(2,1)S(1)} %copy-done), kind=kOutput, calls=%fused_computation | convolution fusion | flops 2419064832 | bytes 10027008 | tf_op jit(solution)/shard_map/dot_general | solution.py:43
  225.8 0.0 reduce-scatter.6.cloned.1.call-update
  225.8 0.0 all-gather.8.cloned.1.call-start
  225.9 0.6 copy-done.3
  226.5 62.3 %reduce-scatter.6.cloned.1.call-done = bf16[256,768]{1,0:T(8,128)(2,1)} async-done(((bf16[4096,768]{1,0:T(8,128)(2,1)}), bf16[256,768]{1,0:T(8,128)(2,1)}) %reduce-scatter.6.cloned.1.call-update) | async-done | bytes 393232 | tf_op jit(solution)/shard_map/reduce_scatter | solution.py:42
  288.8 2.0 fusion.7
  290.8 0.0 all-gather.8.cloned.1.call-update
  290.9 0.0 reduce-scatter.8.cloned.1.call-start
  290.9 48.3 %all-gather.8.cloned.1.call-done = bf16[4096,768]{1,0:T(8,128)(2,1)} async-done(((bf16[256,768]{1,0:T(8,128)(2,1)}), bf16[4096,768]{1,0:T(8,128)(2,1)}) %all-gather.8.cloned.1.call-update) | async-done | bytes 6291472 | tf_op jit(solution)/shard_map/all_gather | solution.py:51
  339.2 7.9 %convolution_convert_fusion.2 = bf16[4096,384]{1,0:T(8,128)(2,1)} fusion(bf16[4096,768]{1,0:T(8,128)(2,1)} %all-gather.8.cloned.1.call-done, bf16[768,384]{1,0:T(8,128)(2,1)S(1)} %copy-done.8), kind=kOutput, calls=%fused_computation.2 | convolution fusion | flops 2417491968 | bytes 10027008 | tf_op jit(solution)/shard_map/dot_general | solution.py:54
  347.1 0.0 reduce-scatter.8.cloned.1.call-update
  347.2 0.7 copy-done.7
  347.8 76.8 %reduce-scatter.8.cloned.1.call-done = bf16[256,384]{1,0:T(8,128)(2,1)} async-done(((bf16[4096,384]{1,0:T(8,128)(2,1)}), bf16[256,384]{1,0:T(8,128)(2,1)}) %reduce-scatter.8.cloned.1.call-update) | async-done | bytes 196624 | tf_op jit(solution)/shard_map/reduce_scatter | solution.py:53
  424.7 1.7 add_convert_fusion
  (18 shorter events, 0.0 us)
Async XLA Ops:
  6.5 211.3 %copy-start = (bf16[384,768]{1,0:T(8,128)(2,1)S(1)}, bf16[384,768]{1,0:T(8,128)(2,1)}, u32[]{:S(2)}) copy-start(bf16[384,768]{1,0:T(8,128)(2,1)} %param.16) | copy-start | bytes 1769476
  6.5 47.9 %all-gather.4.cloned.1.call-start = ((), (), s32[]{:S(2)}) async-start(), calls=%async_computation.3 | async-start | bytes 3342336 | tf_op jit(solution)/shard_map/all_gather | solution.py:21
  7.3 130.3 %reduce-scatter.4.cloned.1.call-start = ((), (), s32[]{:S(2)}) async-start(), calls=%async_computation.4 | async-start | bytes 3342336 | tf_op jit(solution)/shard_map/reduce_scatter | solution.py:23
  60.0 0.7 copy-start.4
  60.0 0.7 copy-start.5
  60.0 0.7 copy-start.6
  60.0 77.6 %copy-start.1 = (bf16[256,384]{1,0:T(8,128)(2,1)S(1)}, bf16[256,384]{1,0:T(8,128)(2,1)}, u32[]{:S(2)}) copy-start(bf16[256,384]{1,0:T(8,128)(2,1)} %param.11) | copy-start | bytes 589828
  60.0 157.8 %all-gather.6.cloned.1.call-start = ((), (), s32[]{:S(2)}) async-start(), calls=%async_computation.5 | async-start | bytes 3342336 | tf_op jit(solution)/shard_map/all_gather | solution.py:40
  166.2 122.6 %reduce-scatter.6.cloned.1.call-start = ((), (), s32[]{:S(2)}) async-start(), calls=%async_computation.6 | async-start | bytes 6684672 | tf_op jit(solution)/shard_map/reduce_scatter | solution.py:42
  225.8 0.7 copy-start.3
  225.8 113.4 %copy-start.8 = (bf16[768,384]{1,0:T(8,128)(2,1)S(1)}, bf16[768,384]{1,0:T(8,128)(2,1)}, u32[]{:S(2)}) copy-start(bf16[768,384]{1,0:T(8,128)(2,1)} %param.18) | copy-start | bytes 1769476
  225.8 113.3 %all-gather.8.cloned.1.call-start = ((), (), s32[]{:S(2)}) async-start(), calls=%async_computation.7 | async-start | bytes 6684672 | tf_op jit(solution)/shard_map/all_gather | solution.py:51
  290.9 133.8 %reduce-scatter.8.cloned.1.call-start = ((), (), s32[]{:S(2)}) async-start(), calls=%async_computation.8 | async-start | bytes 3342336 | tf_op jit(solution)/shard_map/reduce_scatter | solution.py:53
  347.1 0.7 copy-start.7
  347.1 77.5 %copy-start.2 = (bf16[256,384]{1,0:T(8,128)(2,1)S(1)}, bf16[256,384]{1,0:T(8,128)(2,1)}, u32[]{:S(2)}) copy-start(bf16[256,384]{1,0:T(8,128)(2,1)} %reduce-scatter.4.cloned.1.call-done) | copy-start | bytes 589828
Sparse Core Ops, SparseCore 0:
  9.2 45.1 all-gather.3
  60.2 77.3 reduce-scatter.3
  166.3 51.4 all-gather.5
  226.0 62.7 reduce-scatter.5
  291.0 48.1 all-gather.7
  347.3 77.3 reduce-scatter.7
where the time goes:
time: 434 us; the launch traced here: 433 us
  waiting for transfers between devices  364 us (84%)
  blocking collectives  25.7 us (6%)
  matrix products  21.5 us (5%)
  between operations  13.5 us (3%)
  other arithmetic  6.65 us (2%)
    reduce_scatter x1, waiting for transfers between devices, local(): lax.psum_scatter(jnp.dot(rows_part, proj_weight, preferred_element_type=j...  76.8 us
    reduce_scatter x1, waiting for transfers between devices, local(): lax.psum_scatter(jnp.dot(rows_part, down_weight, preferred_element_type=j...  76.8 us
    reduce_scatter x1, waiting for transfers between devices, local(): lax.psum_scatter(jnp.dot(rows_part, up_weight, preferred_element_type=jnp...  62.3 us
    all_gather x1, waiting for transfers between devices, local(): normed_all = lax.all_gather(normed, 'col', axis=0, tiled=True)  51.6 us
    all_gather x1, waiting for transfers between devices, local(): hidden_all = lax.all_gather(hidden_local, 'row', axis=0, tiled=True)  48.3 us
    all_gather x1, waiting for transfers between devices, local(): context_all = lax.all_gather(context, 'row', axis=0, tiled=True)  47.1 us
    psum x1, blocking collectives, local(): lax.psum((jnp.sum(mixed, axis=1, keepdims=True), jnp.sum(mixed * mixed, a...  25.7 us
  transfers between devices with their start and end apart: 6, of which 6 were waited for; matrix products, arithmetic and copies ran while one was open for 0% of the time, Pallas kernels for 0%

commit v1 on v0

v1 whole, which is shorter than its diff:
```python
import functools

import jax
import jax.numpy as jnp
from jax import lax
from jax.experimental import pallas as pl
from jax.experimental.pallas import tpu as pltpu
from jax.sharding import PartitionSpec as P

D = 6144
F = 384
S = 4
T = 128 // S
NZ, NX, NY = 8, 4, 4
MESH = pl.DeviceIdType.MESH
STARTS = (
    ("spread", 0.0, 1.0),
    ("project", 6.0, 12.0),
    ("reduce_mid", 10.0, 12.0),
    ("mix", 14.0, 12.0),
    ("norm", 18.0, 12.0),
    ("forward", 22.0, 12.0),
    ("up", 26.0, 12.0),
    ("gelu", 36.0, 12.0),
    ("down", 46.0, 12.0),
    ("reduce_out", 51.0, 12.0),
    ("finish", 56.0, 12.0),
)
SLOTS = {"spread": 0, "project": 7, "reduce_mid": 13, "mix": 19, "norm": 26, "forward": 32, "up": 38, "gelu": 45,
         "down": 52, "reduce_out": 58, "finish": 64, "swap": 65}
N_SLOTS = 66


def kernel(ctx, res, wp, pb, ng, ns, wu, ub, wd, db, out,
           ctx_all, wproj, wup, wdown, resb, vec, att, rs1, red, rs2, mixed, st, nrm, prep, zr, hid,
           outp, os1, ored, os2, obuf, ssem, rsem, wssem, wrsem, lsem):
    r, q = lax.axis_index("row"), lax.axis_index("col")
    z, c = r // 2, r % 2
    x, y = q // 4, q % 4
    sib = (z * 2 + 1 - c, q)

    def zi(d):
        return (z + d) % NZ

    def xi(d):
        return (x + d) % NX

    def yi(d):
        return (y + d) % NY

    def zp(d):
        return (zi(d) * 2 + c, q)

    def xp(d):
        return (r, xi(d) * 4 + y)

    def yp(d):
        return (r, x * 4 + yi(d))

    barrier = pltpu.get_barrier_semaphore()
    partners = [sib] + [zp(d) for d in range(1, NZ)] + [xp(d) for d in range(1, NX)] + [yp(d) for d in range(1, NY)]
    for p in partners:
        pl.semaphore_signal(barrier, inc=1, device_id=p, device_id_type=MESH)
    pl.semaphore_wait(barrier, len(partners))

    started = []

    def remote(src, dst, send, recv, device):
        copy = pltpu.make_async_remote_copy(
            src_ref=src, dst_ref=dst, send_sem=send, recv_sem=recv, device_id=device, device_id_type=MESH
        )
        copy.start()
        started.append(copy)
        return copy

    def local(src, dst, sem):
        copy = pltpu.make_async_copy(src, dst, sem)
        copy.start()
        return copy

    def rows(start, size):
        return pl.ds(pl.multiple_of(start, 16), size)

    mine = pl.ds(pl.multiple_of(c * F, 128), F)
    my_rows = rows(c * F, F)
    ctx_in = {}
    for s in range(S):
        ctx_in[s] = (
            remote(ctx.at[rows((1 - c) * 128 + s * T, T)], ctx_all.at[s, z, c],
                   ssem.at[s, SLOTS["swap"]], rsem.at[s, SLOTS["swap"]], sib),
            local(ctx.at[rows(c * 128 + s * T, T)], ctx_all.at[s, z, c], lsem.at[s]),
        )
    vec[c, 0:1, :] = pb[...].astype(jnp.float32)
    vec[c, 1:2, :] = ng[...].astype(jnp.float32)
    vec[c, 2:3, :] = ns[...].astype(jnp.float32)
    vec[c, 3:4, :] = db[...].astype(jnp.float32)
    w_in = {
        "proj": (remote(wp, wproj.at[:, mine], wssem.at[0], wrsem.at[0], sib), local(wp, wproj.at[:, mine], lsem.at[S])),
        "res": (
            remote(res.at[rows((1 - c) * 128, 128)], resb.at[c], wssem.at[1], wrsem.at[1], sib),
            local(res.at[rows(c * 128, 128)], resb.at[c], lsem.at[S + 1]),
        ),
        "vec": (remote(vec.at[c], vec.at[c], wssem.at[2], wrsem.at[2], sib),),
        "up": (remote(wu, wup.at[my_rows], wssem.at[3], wrsem.at[3], sib), local(wu, wup.at[my_rows], lsem.at[S + 2])),
        "down": (remote(wd, wdown.at[:, mine], wssem.at[4], wrsem.at[4], sib), local(wd, wdown.at[:, mine], lsem.at[S + 3])),
    }

    def ready(name):
        if name in w_in:
            copies = w_in.pop(name)
            copies[0].wait_recv()
            for copy in copies[1:]:
                copy.wait()

    flights = {}

    def send(name, s, moves):
        base = SLOTS[name]
        flights[name, s] = [
            remote(src, dst, ssem.at[s, base + i], rsem.at[s, base + i], device)
            for i, (src, dst, device) in enumerate(moves)
        ]

    def arrive(name, s):
        for copy in flights[name, s]:
            copy.wait_recv()

    def spread(s):
        ctx_in[s][0].wait_recv()
        ctx_in[s][1].wait()
        send("spread", s, [(ctx_all.at[s, z], ctx_all.at[s, z], zp(d)) for d in range(1, NZ)])

    def scatter_first(name, s, product, part, landing):
        product = product.astype(jnp.bfloat16)
        part[s, 0] = product[:, :F].reshape(NX, NY, T, F)
        for i in range(NX):
            for j in range(NY):
                part[s, 1, j, i] = product[(i * NY + j) * T:(i * NY + j + 1) * T, F:]
        send(name, s, [(part.at[s, 0, xi(d)], landing.at[s, 0, d - 1], xp(d)) for d in range(1, NX)]
             + [(part.at[s, 1, yi(d)], landing.at[s, 1, d - 1], yp(d)) for d in range(1, NY)])

    def scatter_second(source, name, s, part, landing, reduced, landing2):
        arrive(source, s)
        for h, own in ((0, x), (1, y)):
            total = part[s, h, own].astype(jnp.float32)
            for d in range(3):
                total = total + landing[s, h, d].astype(jnp.float32)
            reduced[s, h] = total.astype(jnp.bfloat16)
        send(name, s, [(reduced.at[s, 0, yi(d)], landing2.at[s, 0, d - 1], yp(d)) for d in range(1, NY)]
             + [(reduced.at[s, 1, xi(d)], landing2.at[s, 1, d - 1], xp(d)) for d in range(1, NX)])

    def scattered(source, s, reduced, landing2):
        arrive(source, s)
        totals = []
        for h, own in ((0, y), (1, x)):
            total = reduced[s, h, own].astype(jnp.float32)
            for d in range(3):
                total = total + landing2[s, h, d].astype(jnp.float32)
            totals.append(total)
        return totals

    def project(s):
        arrive("spread", s)
        ready("proj")
        product = jnp.dot(ctx_all[s].reshape(16 * T, F), wproj[...], preferred_element_type=jnp.float32)
        scatter_first("project", s, product, att, rs1)

    def reduce_mid(s):
        scatter_second("project", "reduce_mid", s, att, rs1, red, rs2)

    def mix(s):
        totals = scattered("reduce_mid", s, red, rs2)
        ready("res")
        ready("vec")
        row_sum, row_square = 0.0, 0.0
        for h in range(2):
            value = resb[h, s * T:(s + 1) * T, :].astype(jnp.float32) + totals[h] + vec[h, 0:1, :]
            mixed[s, h] = value
            row_sum = row_sum + jnp.sum(value, axis=1, keepdims=True)
            row_square = row_square + jnp.sum(value * value, axis=1, keepdims=True)
        lane = lax.broadcasted_iota(jnp.int32, (T, 128), 1)
        st[s, z] = jnp.where(lane < 64, row_sum, row_square)
        send("mix", s, [(st.at[s, z], st.at[s, z], zp(d)) for d in range(1, NZ)])

    def norm(s):
        arrive("mix", s)
        total = jnp.sum(st[s], axis=0)
        mean = total[:, 0:1] / D
        var = total[:, 64:65] / D - mean * mean
        scale = lax.rsqrt(var + 1e-05)
        for h in range(2):
            normed = (mixed[s, h] - mean) * scale * vec[h, 1:2, :] + vec[h, 2:3, :]
            nrm[s, x, y, :, h * F:(h + 1) * F] = normed.astype(jnp.bfloat16)
        left, right = nrm.at[s, x, y, :, 0:F], nrm.at[s, x, y, :, F:2 * F]
        send("norm", s, [(left, left, xp(d)) for d in range(1, NX)] + [(right, right, yp(d)) for d in range(1, NY)])

    def forward(s):
        arrive("norm", s)
        left, right = nrm.at[s, :, y, :, 0:F], nrm.at[s, x, :, :, F:2 * F]
        send("forward", s, [(left, left, yp(d)) for d in range(1, NY)] + [(right, right, xp(d)) for d in range(1, NX)])

    def up(s):
        arrive("forward", s)
        ready("up")
        product = jnp.dot(nrm[s].reshape(16 * T, 2 * F), wup[...], preferred_element_type=jnp.float32)
        prep[s] = product.astype(jnp.bfloat16).reshape(NZ, 2 * T, 2 * F)
        send("up", s, [(prep.at[s, zi(d)], zr.at[s, d - 1], zp(d)) for d in range(1, NZ)])

    def gelu(s):
        arrive("up", s)
        total = prep[s, z].astype(jnp.float32) + ub[...].astype(jnp.float32)
        for d in range(7):
            total = total + zr[s, d].astype(jnp.float32)
        hid[s, z] = jax.nn.gelu(total, approximate=True).astype(jnp.bfloat16)
        send("gelu", s, [(hid.at[s, z], hid.at[s, z], zp(d)) for d in range(1, NZ)])

    def down(s):
        arrive("gelu", s)
        ready("down")
        product = jnp.dot(hid[s].reshape(16 * T, 2 * F), wdown[...], preferred_element_type=jnp.float32)
        scatter_first("down", s, product, outp, os1)

    def reduce_out(s):
        scatter_second("down", "reduce_out", s, outp, os1, ored, os2)

    out_local = []

    def finish(s):
        totals = scattered("reduce_out", s, ored, os2)
        for h in range(2):
            obuf[s, h] = (mixed[s, h] + totals[h] + vec[h, 3:4, :]).astype(jnp.bfloat16)
        place = out.at[rows(c * 128 + s * T, T)]
        send("finish", s, [(obuf.at[s, 1 - c], place, sib)])
        out_local.append(local(obuf.at[s, c], place, lsem.at[s]))

    stages = dict(spread=spread, project=project, reduce_mid=reduce_mid, mix=mix, norm=norm, forward=forward,
                  up=up, gelu=gelu, down=down, reduce_out=reduce_out, finish=finish)
    order = sorted((start + s * gap, place, s, name) for place, (name, start, gap) in enumerate(STARTS) for s in range(S))
    for _, _, s, name in order:
        stages[name](s)
    for s in range(S):
        arrive("finish", s)
    for copy in out_local:
        copy.wait()
    for copy in started:
        copy.wait_send()


def local_step(context, residual_in, proj_weight, proj_bias, norm_gain, norm_shift, up_weight, up_bias, down_weight, down_bias):
    bf16, f32 = jnp.bfloat16, jnp.float32
    vmem, hbm = pl.BlockSpec(memory_space=pltpu.VMEM), pl.BlockSpec(memory_space=pl.ANY)
    return pl.pallas_call(
        kernel,
        out_shape=jax.ShapeDtypeStruct((256, F), bf16),
        in_specs=[hbm, hbm, hbm, vmem, vmem, vmem, hbm, vmem, hbm, vmem],
        out_specs=hbm,
        scratch_shapes=[
            pltpu.VMEM((S, NZ, 2, T, F), bf16),
            pltpu.VMEM((F, 2 * F), bf16),
            pltpu.VMEM((2 * F, 2 * F), bf16),
            pltpu.VMEM((2 * F, 2 * F), bf16),
            pltpu.VMEM((2, 128, F), bf16),
            pltpu.VMEM((2, 8, F), f32),
            pltpu.VMEM((S, 2, 4, 4, T, F), bf16),
            pltpu.VMEM((S, 2, 3, 4, T, F), bf16),
            pltpu.VMEM((S, 2, 4, T, F), bf16),
            pltpu.VMEM((S, 2, 3, T, F), bf16),
            pltpu.VMEM((S, 2, T, F), f32),
            pltpu.VMEM((S, NZ, T, 128), f32),
            pltpu.VMEM((S, NX, NY, T, 2 * F), bf16),
            pltpu.VMEM((S, NZ, 2 * T, 2 * F), bf16),
            pltpu.VMEM((S, NZ - 1, 2 * T, 2 * F), bf16),
            pltpu.VMEM((S, NZ, 2 * T, 2 * F), bf16),
            pltpu.VMEM((S, 2, 4, 4, T, F), bf16),
            pltpu.VMEM((S, 2, 3, 4, T, F), bf16),
            pltpu.VMEM((S, 2, 4, T, F), bf16),
            pltpu.VMEM((S, 2, 3, T, F), bf16),
            pltpu.VMEM((S, 2, T, F), bf16),
            pltpu.SemaphoreType.DMA((S, N_SLOTS)),
            pltpu.SemaphoreType.DMA((S, N_SLOTS)),
            pltpu.SemaphoreType.DMA((5,)),
            pltpu.SemaphoreType.DMA((5,)),
            pltpu.SemaphoreType.DMA((S + 4,)),
        ],
        compiler_params=pltpu.CompilerParams(
            collective_id=0, has_side_effects=True, vmem_limit_bytes=56 * 2**20
        ),
        name="layer",
    )(context, residual_in, proj_weight, proj_bias.reshape(1, F), norm_gain.reshape(1, F), norm_shift.reshape(1, F),
      up_weight, up_bias.reshape(1, 2 * F), down_weight, down_bias.reshape(1, F))


def solution(mesh):
    return jax.shard_map(
        local_step,
        mesh=mesh,
        in_specs=(
            P("row", "col"),
            P("col", "row"),
            P("col", "row"),
            P("row"),
            P("row"),
            P("row"),
            P("row", "col"),
            P("col"),
            P("col", "row"),
            P("row"),
        ),
        out_specs=P("col", "row"),
        check_vma=False,
    )
```

time: 434 us -> 245 us (0.56)
  waiting for transfers between devices: 364 us -> 0 us
  Pallas kernels: 0 us -> 239 us
  blocking collectives: 25.7 us -> 0 us
  matrix products: 21.5 us -> 0 us
  between operations: 13.5 us -> 0.02 us
  other arithmetic: 6.65 us -> 0 us
    pallas_call x0 -> x1, Pallas kernels: none -> 239 us  [local_step(): pl.pallas_call(kernel, out_shape=jax.ShapeDtypeStruct((256, F), bf16), in...]
    reduce_scatter x3 -> x0, waiting for transfers between devices: 216 us -> none  [the longest x1 76.8 us: local(): lax.psum_scatter(jnp.dot(rows_part, proj_weight, preferred_element_type=j...]
    all_gather x3 -> x0, waiting for transfers between devices: 147 us -> none  [the longest x1 51.6 us: local(): normed_all = lax.all_gather(normed, 'col', axis=0, tiled=True)]
    psum x1 -> x0, blocking collectives: 25.7 us -> none  [local(): lax.psum((jnp.sum(mixed, axis=1, keepdims=True), jnp.sum(mixed * mixed, a...]
    dot_general x3 -> x0, matrix products: 21.5 us -> none  [the longest x1 7.97 us: local(): jnp.dot(rows_part, up_weight, preferred_element_type=jnp.float32)]
    convert_element_type x8 -> x0, other arithmetic: 5.53 us -> none  [the longest x1 2.05 us: local(): jax.nn.gelu(pre_local + up_bias.astype(jnp.float32), approximate=True)]
  transfers between devices with their start and end apart: 6 -> 0, of which waited for: 6 -> 0; matrix products, arithmetic and copies ran while one was open for 0% -> 0% of each run, Pallas kernels for 0% -> 0%
where the time goes in v1:
time: 245 us
  Pallas kernels  239 us (98%)
  local copies, waits for them, and re-layouts  5.35 us (2%)
    pallas_call x1, Pallas kernels, local_step(): pl.pallas_call(kernel, out_shape=jax.ShapeDtypeStruct((256, F), bf16), in...  239 us

profile of v1, /device:TPU:1, one launch (start us, length us, event | category | flops | bytes accessed | tf_op | source)
XLA Modules:
  0.0 244.6 jit_solution(106461104595097401)
XLA Ops:
  0.0 0.0 copy-start.1
  0.0 1.3 reshape.15.pb
  1.3 0.0 copy-done.1
  1.3 0.0 copy-start.2
  1.3 0.0 copy-start.3
  1.3 0.6 reshape.16.ng
  1.9 0.1 copy-done.2
  2.0 0.0 copy-start
  2.0 0.6 reshape.17.ns
  2.6 0.0 copy-done.3
  2.6 0.6 reshape.19.db
  3.1 0.0 copy-done
  3.1 0.6 reshape.18.ub
  3.7 239.2 %layer.1 = bf16[256,384]{1,0:T(8,128)(2,1)} custom-call(bf16[256,384]{1,0:T(8,128)(2,1)} %ctx.1, bf16[256,384]{1,0:T(8,128)(2,1)} %res.1, bf16[384,384]{1,0:T(8,128)(2,1)} %wp.1, bf16[1,384]{1,0:T(2,128)(2,1)} %reshape.15.pb, bf16[1,384]{1,0:T(2,128)(2,1)} %reshape.16.ng, bf16[1,384]{1,0:T(2,128)(2,1)} %reshape.17.ns, bf16[384,768]{1,0:T(8,128)(2,1)} %wu.1, ...), custom_call_target="tpu_custom_call" | custom-call | tf_op jit(solution)/shard_map/layer/pallas_call | solution.py:252
  243.0 1.6 copy.12
Async XLA Ops:
  0.0 1.3 copy-start.1
  1.3 0.7 copy-start.2
  1.3 1.3 copy-start.3
  2.0 1.2 copy-start

commit v2 on v0

v2 whole, which is shorter than its diff:
```python
import jax
import jax.numpy as jnp
from jax import lax
from jax.experimental import pallas as pl
from jax.experimental.pallas import tpu as pltpu
from jax.sharding import PartitionSpec as P

D = 6144
F = 384
H = 128
CHUNKS = (32, 32, 32, 32)
GROUPS = ((1,), (2, 3))
S = len(CHUNKS)
OFFSETS = tuple(sum(CHUNKS[:s]) for s in range(S))
NZ, NX, NY = 8, 4, 4
MESH = pl.DeviceIdType.MESH

RING = tuple((2, "z", 3072 * part, 2.2) for part in (1, 1, 1, 0.5))
CHAIN = (
    ("project", 6, "xy", 6144, 2.8, 0.016),
    ("reduce_mid", 6, "xy", 1536, 2.8, 0.01),
    ("mix", 7, "z", 0, 4.0, 0.01),
    ("norm", 6, "xy", 1536, 2.8, 0.01),
    ("forward", 6, "xy", 6144, 2.8, 0.0),
    ("up", 2, "z", 1536, 2.2, 0.024),
    ("pass1", 2, "z", 3072, 2.2, 0.008),
    ("pass2", 2, "z", 3072, 2.2, 0.008),
    ("pass3", 2, "z", 3072, 2.2, 0.008),
    ("gelu", 2, "z", 3072, 2.2, 0.016),
    ("hand1", 2, "z", 3072, 2.2, 0.0),
    ("hand2", 2, "z", 3072, 2.2, 0.0),
    ("hand3", 2, "z", 1536, 2.2, 0.0),
    ("down", 6, "xy", 6144, 2.8, 0.024),
    ("reduce_out", 6, "xy", 1536, 2.8, 0.01),
    ("finish", 1, "core", 0, 1.0, 0.01),
)
RATE = 65000.0


def issue_order():
    ring = tuple(("ctx%d" % t, 2, "z", 1536 * (0.5 if t == 3 else 1), 2.2, 0.0) for t in range(4))
    chains = [[("spread", 7, "z", 12288, 4.0, 0.0, 0, CHUNKS[0])] + [st + (0, CHUNKS[0]) for st in CHAIN]]
    chains += [[st + (s, CHUNKS[s]) for st in CHAIN] for s in range(1, S)]
    for g, members in enumerate(GROUPS):
        chains.append([st + (g, sum(CHUNKS[s] for s in members)) for st in ring])
    waits = {s: S + g for g, members in enumerate(GROUPS) for s in members}
    place, ready = [0] * len(chains), [0.0] * len(chains)
    for s in range(1, S):
        ready[s] = float("inf")
    free, now, order = {"z": 0.0, "xy": 0.0, "core": 0.0}, 0.0, []
    while any(p < len(ch) for p, ch in zip(place, chains)):
        live = [i for i in range(len(chains)) if place[i] < len(chains[i])]
        first = min(ready[i] for i in live)
        due = [i for i in live if ready[i] <= max(now, first)]
        i = min(due)
        name, copies, link, size, latency, work, index, tokens = chains[i][place[i]]
        now = max(now, ready[i]) + work * tokens + 0.06 * copies
        free[link] = max(free[link], now) + size * tokens / RATE
        ready[i] = free[link] + latency
        place[i] += 1
        order.append((name, index))
        if i >= S and place[i] == len(chains[i]):
            for s, chain in waits.items():
                if chain == i:
                    ready[s] = ready[i]
    return order, max(ready[:S])


def kernel(ctx, res, wp, pb, ng, ns, wu, ub, wd, db, out,
           ctx_all, wproj, wup, wdown, resb, vin0, vin1, vin2, vin3, uin, vec, att, rs1, red, rs2, mixed, st, nrm, prep, zr, hid,
           outp, os1, ored, os2, obuf, ssem, rsem, wssem, wrsem, lsem):
    r, q = lax.axis_index("row"), lax.axis_index("col")
    z, c = r // 2, r % 2
    x, y = q // 4, q % 4
    sib = (z * 2 + 1 - c, q)

    def zi(d):
        return (z + d + NZ) % NZ

    def xi(d):
        return (x + d) % NX

    def yi(d):
        return (y + d) % NY

    def zp(d):
        return (zi(d) * 2 + c, q)

    def xp(d):
        return (r, xi(d) * 4 + y)

    def yp(d):
        return (r, x * 4 + yi(d))

    def rows(start, size):
        return pl.ds(pl.multiple_of(start, 16), size)

    def local(src, dst, sem):
        copy = pltpu.make_async_copy(src, dst, sem)
        copy.start()
        return copy

    sends = []

    def remote(src, dst, send, recv, device):
        copy = pltpu.make_async_remote_copy(
            src_ref=src, dst_ref=dst, send_sem=send, recv_sem=recv, device_id=device, device_id_type=MESH
        )
        copy.start()
        sends.append(copy)
        return copy

    vin = (vin0, vin1, vin2, vin3)
    mine = pl.ds(pl.multiple_of(c * F, 128), F)
    my_rows = rows(c * F, F)
    near, far = c * H, (1 - c) * H
    early = CHUNKS[0]
    own = {
        "first": [local(ctx.at[rows(near, early)], ctx_all.at[z, c, 0:early], lsem.at[0])],
        "vec": [local(v, vin[i], lsem.at[1 + i]) for i, v in enumerate((pb, ng, ns, db))],
        "rest": [local(ctx.at[rows(near + early, H - early)], ctx_all.at[z, c, early:H], lsem.at[5])],
        "proj": [local(wp, wproj.at[:, mine], lsem.at[6])],
        "res": [local(res.at[rows(near, H)], resb.at[c], lsem.at[7])],
        "up": [local(wu, wup.at[my_rows], lsem.at[8]), local(ub, uin, lsem.at[9])],
        "down": [local(wd, wdown.at[:, mine], lsem.at[10])],
    }
    barrier = pltpu.get_barrier_semaphore()
    partners = [sib] + [zp(d) for d in range(1, NZ)] + [xp(d) for d in range(1, NX)] + [yp(d) for d in range(1, NY)]
    for p in partners:
        pl.semaphore_signal(barrier, inc=1, device_id=p, device_id_type=MESH)
    pl.semaphore_wait(barrier, len(partners))

    def swap(i, src, dst):
        return remote(src, dst, wssem.at[i], wrsem.at[i], sib)

    theirs = {
        "first": swap(0, ctx.at[rows(far, early)], ctx_all.at[z, c, 0:early]),
        "rest": swap(1, ctx.at[rows(far + early, H - early)], ctx_all.at[z, c, early:H]),
        "proj": swap(2, wp, wproj.at[:, mine]),
        "res": swap(3, res.at[rows(far, H)], resb.at[c]),
    }
    for copy in own.pop("vec"):
        copy.wait()
    for i in range(4):
        vec[c, i:i + 1, :] = vin[i][...].reshape(1, F).astype(jnp.float32)
    theirs["vec"] = swap(4, vec.at[c], vec.at[c])
    theirs["up"] = swap(5, wu, wup.at[my_rows])
    theirs["down"] = swap(6, wd, wdown.at[:, mine])

    def ready(name):
        if name in theirs:
            theirs.pop(name).wait_recv()
            for copy in own.pop(name, ()):
                copy.wait()

    flights, slots = {}, {}

    def send(name, s, moves):
        copies = []
        for src, dst, device in moves:
            i = slots[s] = slots.get(s, -1) + 1
            copies.append(remote(src, dst, ssem.at[s, i], rsem.at[s, i], device))
        flights[name, s] = copies

    def arrive(name, s):
        for copy in flights[name, s]:
            copy.wait_recv()

    def clear(keep):
        while len(sends) > keep:
            sends.pop(0).wait_send()

    def part(s):
        return slice(OFFSETS[s], OFFSETS[s] + CHUNKS[s])

    def spread(s):
        ready("first")
        piece = ctx_all.at[z, :, part(0), :]
        send("spread", 0, [(piece, piece, zp(d)) for d in (4, 3, 5, 2, 6, 1, 7)])

    def ring(t):
        def step(g):
            members = GROUPS[g]
            span = slice(OFFSETS[members[0]], OFFSETS[members[-1]] + CHUNKS[members[-1]])
            if t == 0:
                ready("rest")
            else:
                arrive("ctx%d" % (t - 1), S + g)
            blocks = (0, 1) if t == 3 else (slice(0, 2), slice(0, 2))
            up_piece, down_piece = ctx_all.at[zi(-t), blocks[0], span, :], ctx_all.at[zi(t), blocks[1], span, :]
            send("ctx%d" % t, S + g, [(up_piece, up_piece, zp(1)), (down_piece, down_piece, zp(-1))])
        return step

    def scatter_first(name, s, product, piece, landing):
        product, k, t = product.astype(jnp.bfloat16), part(s), CHUNKS[s]
        piece[0, :, :, k, :] = product[:, :F].reshape(NX, NY, t, F)
        for i in range(NX):
            for j in range(NY):
                piece[1, j, i, k, :] = product[(i * NY + j) * t:(i * NY + j + 1) * t, F:]
        send(name, s, [
            move
            for d in (1, 3, 2)
            for move in (
                (piece.at[0, xi(d), :, k, :], landing.at[0, d - 1, :, k, :], xp(d)),
                (piece.at[1, yi(d), :, k, :], landing.at[1, d - 1, :, k, :], yp(d)),
            )
        ])

    def scatter_second(source, name, s, piece, landing, reduced, landing2):
        arrive(source, s)
        k = part(s)
        for h, own_at in ((0, x), (1, y)):
            total = piece[h, own_at, :, k, :].astype(jnp.float32)
            for d in range(3):
                total = total + landing[h, d, :, k, :].astype(jnp.float32)
            reduced[h, :, k, :] = total.astype(jnp.bfloat16)
        send(name, s, [
            move
            for d in (1, 3, 2)
            for move in (
                (reduced.at[0, yi(d), k, :], landing2.at[0, d - 1, k, :], yp(d)),
                (reduced.at[1, xi(d), k, :], landing2.at[1, d - 1, k, :], xp(d)),
            )
        ])

    def scattered(source, s, reduced, landing2):
        arrive(source, s)
        k, totals = part(s), []
        for h, own_at in ((0, y), (1, x)):
            total = reduced[h, own_at, k, :].astype(jnp.float32)
            for d in range(3):
                total = total + landing2[h, d, k, :].astype(jnp.float32)
            totals.append(total)
        return totals

    def project(s):
        if s == 0:
            arrive("spread", 0)
        else:
            g = [s in members for members in GROUPS].index(True)
            if ("ctx3", S + g) in flights:
                arrive("ctx3", S + g)
                del flights["ctx3", S + g]
        ready("proj")
        product = jnp.dot(ctx_all[:, :, part(s), :].reshape(16 * CHUNKS[s], F), wproj[...], preferred_element_type=jnp.float32)
        scatter_first("project", s, product, att, rs1)

    def reduce_mid(s):
        scatter_second("project", "reduce_mid", s, att, rs1, red, rs2)

    def mix(s):
        totals = scattered("reduce_mid", s, red, rs2)
        ready("res")
        ready("vec")
        k, t = part(s), CHUNKS[s]
        row_sum, row_square = jnp.zeros((t, 128), jnp.float32), jnp.zeros((t, 128), jnp.float32)
        for h in range(2):
            value = resb[h, k, :].astype(jnp.float32) + totals[h] + vec[h, 0:1, :]
            mixed[h, k, :] = value
            for i in range(0, F, 128):
                row_sum = row_sum + value[:, i:i + 128]
                row_square = row_square + value[:, i:i + 128] * value[:, i:i + 128]
        pad = jnp.zeros((64 - t, 128), jnp.float32)
        lanes = jnp.concatenate([row_sum, pad, row_square, pad], axis=0).T
        st[s, z] = jnp.sum(lanes, axis=0, keepdims=True)
        send("mix", s, [(st.at[s, z], st.at[s, z], zp(d)) for d in (4, 3, 5, 2, 6, 1, 7)])

    def norm(s):
        arrive("mix", s)
        k, t = part(s), CHUNKS[s]
        total = jnp.broadcast_to(jnp.sum(st[s], axis=0), (128, 128)).T
        mean = total[0:t, 0:1] / D
        var = total[64:64 + t, 0:1] / D - mean * mean
        scale = lax.rsqrt(var + 1e-05)
        for h in range(2):
            normed = (mixed[h, k, :] - mean) * scale * vec[h, 1:2, :] + vec[h, 2:3, :]
            nrm[x, y, k, h * F:(h + 1) * F] = normed.astype(jnp.bfloat16)
        left, right = nrm.at[x, y, k, 0:F], nrm.at[x, y, k, F:2 * F]
        send("norm", s, [move for d in (1, 3, 2) for move in ((left, left, xp(d)), (right, right, yp(d)))])

    def forward(s):
        arrive("norm", s)
        left, right = nrm.at[:, y, part(s), 0:F], nrm.at[x, :, part(s), F:2 * F]
        send("forward", s, [move for d in (1, 3, 2) for move in ((left, left, yp(d)), (right, right, xp(d)))])

    def up(s):
        arrive("forward", s)
        ready("up")
        k, t = part(s), CHUNKS[s]
        product = jnp.dot(nrm[:, :, k, :].reshape(16 * t, 2 * F), wup[...], preferred_element_type=jnp.float32)
        prep[:, :, k, :] = product.astype(jnp.bfloat16).reshape(NZ, 2, t, 2 * F)
        send("up", s, [
            (prep.at[zi(4), 0, k, :], zr.at[0, 0, 0, k, :], zp(1)),
            (prep.at[zi(4), 1, k, :], zr.at[1, 0, 1, k, :], zp(-1)),
        ])

    def add(at, step, way, blocks, k):
        prep[at, blocks, k, :] = (
            prep[at, blocks, k, :].astype(jnp.float32) + zr[way, step, blocks, k, :].astype(jnp.float32)
        ).astype(jnp.bfloat16)

    def passing(t):
        def step(s):
            arrive("up" if t == 1 else "pass%d" % (t - 1), s)
            k = part(s)
            moves = []
            for way, sign in ((0, 1), (1, -1)):
                at = zi(sign * (4 - t))
                add(at, t - 1, way, way if t == 1 else slice(0, 2), k)
                moves.append((prep.at[at, :, k, :], zr.at[way, t, :, k, :], zp(sign)))
            send("pass%d" % t, s, moves)
        return step

    def gelu(s):
        arrive("pass3", s)
        k = part(s)
        total = prep[z, :, k, :].astype(jnp.float32) + zr[0, 3, :, k, :].astype(jnp.float32)
        total = total + zr[1, 3, :, k, :].astype(jnp.float32) + uin[...].reshape(1, 2 * F).astype(jnp.float32)
        hid[z, :, k, :] = jax.nn.gelu(total, approximate=True).astype(jnp.bfloat16)
        piece = hid.at[z, :, k, :]
        send("gelu", s, [(piece, piece, zp(1)), (piece, piece, zp(-1))])

    def handing(t):
        def step(s):
            arrive("gelu" if t == 1 else "hand%d" % (t - 1), s)
            blocks = (0, 1) if t == 3 else (slice(0, 2), slice(0, 2))
            up_piece, down_piece = hid.at[zi(-t), blocks[0], part(s), :], hid.at[zi(t), blocks[1], part(s), :]
            send("hand%d" % t, s, [(up_piece, up_piece, zp(1)), (down_piece, down_piece, zp(-1))])
        return step

    def down(s):
        arrive("hand3", s)
        ready("down")
        product = jnp.dot(hid[:, :, part(s), :].reshape(16 * CHUNKS[s], 2 * F), wdown[...], preferred_element_type=jnp.float32)
        scatter_first("down", s, product, outp, os1)

    def reduce_out(s):
        scatter_second("down", "reduce_out", s, outp, os1, ored, os2)

    out_local = []

    def finish(s):
        totals = scattered("reduce_out", s, ored, os2)
        k = part(s)
        for h in range(2):
            obuf[h, k, :] = (mixed[h, k, :] + totals[h] + vec[h, 3:4, :]).astype(jnp.bfloat16)
        place = out.at[rows(near + OFFSETS[s], CHUNKS[s])]
        send("finish", s, [(obuf.at[1 - c, k, :], place, sib)])
        out_local.append(local(obuf.at[c, k, :], place, lsem.at[11 + s]))

    stages = dict(spread=spread, project=project, reduce_mid=reduce_mid, mix=mix, norm=norm, forward=forward,
                  up=up, gelu=gelu, down=down, reduce_out=reduce_out, finish=finish)
    for t in range(1, 4):
        stages["pass%d" % t], stages["hand%d" % t] = passing(t), handing(t)
    for t in range(4):
        stages["ctx%d" % t] = ring(t)
    for name, index in issue_order()[0]:
        stages[name](index)
        clear(48)
    for s in range(S):
        arrive("finish", s)
    for copy in out_local:
        copy.wait()
    clear(0)


def layer(context, residual_in, proj_weight, proj_bias, norm_gain, norm_shift, up_weight, up_bias, down_weight, down_bias):
    bf16, f32 = jnp.bfloat16, jnp.float32
    hbm = pl.BlockSpec(memory_space=pl.ANY)
    return pl.pallas_call(
        kernel,
        out_shape=jax.ShapeDtypeStruct((2 * H, F), bf16),
        in_specs=[hbm] * 10,
        out_specs=hbm,
        scratch_shapes=[
            pltpu.VMEM((NZ, 2, H, F), bf16),
            pltpu.VMEM((F, 2 * F), bf16),
            pltpu.VMEM((2 * F, 2 * F), bf16),
            pltpu.VMEM((2 * F, 2 * F), bf16),
            pltpu.VMEM((2, H, F), bf16),
            *[pltpu.VMEM((F,), bf16)] * 4,
            pltpu.VMEM((2 * F,), bf16),
            pltpu.VMEM((2, 8, F), f32),
            pltpu.VMEM((2, 4, 4, H, F), bf16),
            pltpu.VMEM((2, 3, 4, H, F), bf16),
            pltpu.VMEM((2, 4, H, F), bf16),
            pltpu.VMEM((2, 3, H, F), bf16),
            pltpu.VMEM((2, H, F), f32),
            pltpu.VMEM((S, NZ, 1, 128), f32),
            pltpu.VMEM((NX, NY, H, 2 * F), bf16),
            pltpu.VMEM((NZ, 2, H, 2 * F), bf16),
            pltpu.VMEM((2, 4, 2, H, 2 * F), bf16),
            pltpu.VMEM((NZ, 2, H, 2 * F), bf16),
            pltpu.VMEM((2, 4, 4, H, F), bf16),
            pltpu.VMEM((2, 3, 4, H, F), bf16),
            pltpu.VMEM((2, 4, H, F), bf16),
            pltpu.VMEM((2, 3, H, F), bf16),
            pltpu.VMEM((2, H, F), bf16),
            pltpu.SemaphoreType.DMA((S + len(GROUPS), 80)),
            pltpu.SemaphoreType.DMA((S + len(GROUPS), 80)),
            pltpu.SemaphoreType.DMA((7,)),
            pltpu.SemaphoreType.DMA((7,)),
            pltpu.SemaphoreType.DMA((11 + S,)),
        ],
        compiler_params=pltpu.CompilerParams(
            collective_id=0, has_side_effects=True, vmem_limit_bytes=56 * 2**20
        ),
        name="layer",
    )(context, residual_in, proj_weight, proj_bias, norm_gain, norm_shift, up_weight, up_bias, down_weight, down_bias)


def solution(mesh):
    return jax.shard_map(
        layer,
        mesh=mesh,
        in_specs=(
            P("row", "col"),
            P("col", "row"),
            P("col", "row"),
            P("row"),
            P("row"),
            P("row"),
            P("row", "col"),
            P("col"),
            P("col", "row"),
            P("row"),
        ),
        out_specs=P("col", "row"),
        check_vma=False,
    )
```

time: 434 us -> 153 us (0.35)
  waiting for transfers between devices: 364 us -> 0 us
  Pallas kernels: 0 us -> 151 us
  blocking collectives: 25.7 us -> 0 us
  matrix products: 21.5 us -> 0 us
  between operations: 13.5 us -> 0.01 us
  other arithmetic: 6.65 us -> 0 us
    reduce_scatter x3 -> x0, waiting for transfers between devices: 216 us -> none  [the longest x1 76.8 us: local(): lax.psum_scatter(jnp.dot(rows_part, proj_weight, preferred_element_type=j...]
    pallas_call x0 -> x1, Pallas kernels: none -> 151 us  [layer(): pl.pallas_call(kernel, out_shape=jax.ShapeDtypeStruct((2 * H, F), bf16),...]
    all_gather x3 -> x0, waiting for transfers between devices: 147 us -> none  [the longest x1 51.6 us: local(): normed_all = lax.all_gather(normed, 'col', axis=0, tiled=True)]
    psum x1 -> x0, blocking collectives: 25.7 us -> none  [local(): lax.psum((jnp.sum(mixed, axis=1, keepdims=True), jnp.sum(mixed * mixed, a...]
    dot_general x3 -> x0, matrix products: 21.5 us -> none  [the longest x1 7.97 us: local(): jnp.dot(rows_part, up_weight, preferred_element_type=jnp.float32)]
    convert_element_type x8 -> x0, other arithmetic: 5.53 us -> none  [the longest x1 2.05 us: local(): jax.nn.gelu(pre_local + up_bias.astype(jnp.float32), approximate=True)]
  transfers between devices with their start and end apart: 6 -> 0, of which waited for: 6 -> 0; matrix products, arithmetic and copies ran while one was open for 0% -> 0% of each run, Pallas kernels for 0% -> 0%
where the time goes in v2:
time: 153 us
  Pallas kernels  151 us (99%)
  local copies, waits for them, and re-layouts  1.62 us (1%)
    pallas_call x1, Pallas kernels, layer(): pl.pallas_call(kernel, out_shape=jax.ShapeDtypeStruct((2 * H, F), bf16),...  151 us

profile of v2, /device:TPU:1, one launch (start us, length us, event | category | flops | bytes accessed | tf_op | source)
XLA Modules:
  0.0 152.9 jit_solution(11142762676025582624)
XLA Ops:
  0.0 151.2 %layer.1 = bf16[256,384]{1,0:T(8,128)(2,1)} custom-call(bf16[256,384]{1,0:T(8,128)(2,1)} %ctx.1, bf16[256,384]{1,0:T(8,128)(2,1)} %res.1, bf16[384,384]{1,0:T(8,128)(2,1)} %wp.1, bf16[384]{0:T(512)(128)(2,1)} %pb.1, bf16[384]{0:T(512)(128)(2,1)} %ng.1, bf16[384]{0:T(512)(128)(2,1)} %ns.1, bf16[384,768]{1,0:T(8,128)(2,1)} %wu.1, bf16[768]{0:T(1024)(128)(2,1)} %ub.1, ...), custom_call_target="tpu_custom_call" | custom-call | tf_op jit(solution)/shard_map/layer/pallas_call | solution.py:370
  151.2 1.6 %copy.12 = bf16[256,384]{1,0:T(8,128)(2,1)} copy(bf16[256,384]{1,0:T(8,128)(2,1)} %layer.1) | data formatting | bytes 393216

commit v3 on v0

v3 whole, which is shorter than its diff:
```python
import jax
import jax.numpy as jnp
from jax import lax
from jax.experimental import pallas as pl
from jax.experimental.pallas import tpu as pltpu
from jax.sharding import PartitionSpec as P

D = 6144
F = 384
K = 4 * F
U = 8 * F
H = 64
S = 4
T = H // S
GROUPS = ((1,), (2, 3))
NZ, NX, NY = 8, 4, 4
MESH = pl.DeviceIdType.MESH

CHAIN = (
    ("project", 3, "y", 98304, 2.7, 0.6),
    ("mix", 7, "z", 0, 4.3, 0.6),
    ("norm", 3, "y", 98304, 2.7, 0.5),
    ("up", 2, "z", 49152, 2.8, 0.9),
    ("pass1", 2, "z", 98304, 2.8, 0.25),
    ("pass2", 2, "z", 98304, 2.8, 0.25),
    ("pass3", 2, "z", 98304, 2.8, 0.25),
    ("gelu", 2, "z", 98304, 2.8, 0.5),
    ("hand1", 2, "z", 98304, 2.8, 0.0),
    ("hand2", 2, "z", 98304, 2.8, 0.0),
    ("hand3", 2, "z", 49152, 2.8, 0.0),
    ("down", 3, "y", 98304, 2.7, 0.9),
    ("finish", 4, "x", 49152, 2.7, 0.4),
)
RATE = 50000.0
LOADED = {"project": 24.0, "up": 42.0, "down": 62.0}


def issue_order():
    chains = [[("spread", 7, "z", 393216, 4.3, 0.0, 0)] + [st + (0,) for st in CHAIN]]
    chains += [[st + (s,) for st in CHAIN] for s in range(1, S)]
    for g, members in enumerate(GROUPS):
        chains.append([("ctx%d" % t, 2, "z", 49152 * len(members) * (0.5 if t == 3 else 1), 2.8, 0.0, g) for t in range(4)])
    waits = {s: S + g for g, members in enumerate(GROUPS) for s in members}
    place, ready = [0] * len(chains), [16.0] * len(chains)
    for s in range(1, S):
        ready[s] = float("inf")
    free, now, order = {"z": 0.0, "y": 0.0, "x": 0.0}, 0.0, []
    while any(p < len(ch) for p, ch in zip(place, chains)):
        live = [i for i in range(len(chains)) if place[i] < len(chains[i])]
        due_at = {i: max(ready[i], LOADED.get(chains[i][place[i]][0], 0.0)) for i in live}
        first = min(due_at.values())
        i = min(i for i in live if due_at[i] <= max(now, first))
        name, copies, link, size, latency, work, index = chains[i][place[i]]
        now = max(now, due_at[i]) + work + 0.08 * copies
        free[link] = max(free[link], now) + size / RATE
        ready[i] = free[link] + latency
        place[i] += 1
        order.append((name, index))
        if i >= S and place[i] == len(chains[i]):
            for s, chain in waits.items():
                if chain == i:
                    ready[s] = ready[i]
    return order, max(ready[:S])


def kernel(ctx, res, wp, pb, ng, ns, wu, ub, wd, db, out,
           ctx_all, wproj, wup, wdown, resb, vin0, vin1, vin2, vin3, uin, vec, uvec, att, rs, mixed, st, nrm, prep, zr, hid,
           outp, os, obuf, ssem, rsem, wssem, wrsem, csem, gsem, lsem):
    r, q = lax.axis_index("row"), lax.axis_index("col")
    z, c = r // 2, r % 2
    x, y = q // 4, q % 4
    sib = (z * 2 + 1 - c, q)

    def zi(d):
        return (z + d + NZ) % NZ

    def yi(d):
        return (y + d) % NY

    def zp(d):
        return (zi(d) * 2 + c, q)

    def xp(d):
        return (r, ((x + d) % NX) * 4 + y)

    def yp(d):
        return (r, x * 4 + yi(d))

    def rows(start, size):
        return pl.ds(pl.multiple_of(start, 16), size)

    def lanes(start, size):
        return pl.ds(pl.multiple_of(start, 128), size)

    def local(src, dst, sem):
        copy = pltpu.make_async_copy(src, dst, sem)
        copy.start()
        return copy

    sends = []

    def remote(src, dst, send, recv, device):
        copy = pltpu.make_async_remote_copy(
            src_ref=src, dst_ref=dst, send_sem=send, recv_sem=recv, device_id=device, device_id_type=MESH
        )
        copy.start()
        sends.append((None, copy))
        return copy

    def give(src, dst, send, recv, to_core, to_x):
        here = (to_core == c) & (to_x == x)
        copy = pltpu.make_async_remote_copy(
            src_ref=src, dst_ref=dst, send_sem=send, recv_sem=recv, device_id=(z * 2 + to_core, to_x * 4 + y),
            device_id_type=MESH,
        )

        @pl.when(here)
        def _():
            pltpu.make_async_copy(src, dst, recv).start()

        @pl.when(jnp.logical_not(here))
        def _():
            copy.start()

        sends.append((here, copy))

    def clear(keep):
        while len(sends) > keep:
            here, copy = sends.pop(0)
            if here is None:
                copy.wait_send()
            else:
                pl.when(jnp.logical_not(here))(copy.wait_send)

    def landed(ref, sem):
        pltpu.make_async_copy(ref, ref, sem).wait()

    vin = (vin0, vin1, vin2, vin3)
    half = lanes(c * F, F)
    places = {
        "proj": lambda at, core: wproj.at[rows(at * F, F), lanes(core * F, F)],
        "up": lambda at, core: wup.at[rows(core * F, F), lanes(at * 2 * F, 2 * F)],
        "down": lambda at, core: wdown.at[rows(at * 2 * F, 2 * F), lanes(core * F, F)],
    }
    blocks = {"proj": wp, "up": wu, "down": wd}
    vector_in = [local(v, vin[i], lsem.at[i]) for i, v in enumerate((pb, ng, ns, db))] + [local(ub, uin, lsem.at[4])]
    own = {name: local(blocks[name], places[name](x, c), lsem.at[5 + i]) for i, name in enumerate(blocks)}

    barrier = pltpu.get_barrier_semaphore()
    partners = [sib] + [zp(d) for d in range(1, NZ)] + [yp(d) for d in range(1, NY)]
    partners += [p for d in range(1, NX) for p in (xp(d), (sib[0], xp(d)[1]))]
    for p in partners:
        pl.semaphore_signal(barrier, inc=1, device_id=p, device_id_type=MESH)
    pl.semaphore_wait(barrier, len(partners))

    ctx_side = (c + z // 2) % 2
    for g, (low, size) in enumerate(((0, T), (T, H - T))):
        for i in range(2):
            for core in range(2):
                give(ctx.at[rows(128 * core + 64 * i + low, size)], ctx_all.at[z, low:low + size, lanes(x * F, F)],
                     gsem.at[g * 4 + i * 2 + core], csem.at[g], core, 2 * ctx_side + i)
    gathers = {}

    def swap(name, i, src, dst):
        return remote(src, dst, wssem.at[i], wrsem.at[i], sib)

    def gather(name, i):
        mine = places[name](x, c)
        gathers[name] = (
            [remote(blocks[name], mine, wssem.at[8 * i + d], wrsem.at[8 * i + d], xp(d)) for d in (1, 3)],
            [swap(name, 8 * i, blocks[name], mine)],
            [],
            8 * i,
        )

    gather("proj", 0)
    side = (x + y) % 2
    for i in range(2):
        for core in range(2):
            give(res.at[rows(128 * core + 64 * i, H)], resb.at[c, x // 2], gsem.at[8 + i * 2 + core], csem.at[2], core, 2 * side + i)
    for copy in vector_in:
        copy.wait()
    for i in range(4):
        vec[c, i:i + 1, :] = vin[i][...].reshape(1, F).astype(jnp.float32)
    uvec[x, 0:1, :] = uin[...].reshape(1, 2 * F).astype(jnp.float32)
    vec_swap = [swap("vec", 24, vec.at[c], vec.at[c])]
    uvec_gather = [remote(uvec.at[x], uvec.at[x], wssem.at[24 + d], wrsem.at[24 + d], xp(d)) for d in (1, 3, 2)]

    def pass_on(name):
        near, far, relays, i = gathers[name]
        if not relays:
            for copy in near:
                copy.wait_recv()
            for j, (d, to) in enumerate(((-1, 1), (1, 3))):
                place = places[name]((x + d + NX) % NX, c)
                n = place.shape[0] // 2
                piece = place.at[j * n:(j + 1) * n]
                relays.append(remote(piece, piece, wssem.at[i + 4 + j], wrsem.at[i + 4 + j], xp(to)))
            for j, d in enumerate((-1, 1)):
                place = places[name]((x + d + NX) % NX, c)
                far.append(swap(name, i + (2, 6)[j], place, place))

    def pass_far(name):
        near, far, relays, i = gathers[name]
        if len(far) == 3:
            for copy in relays:
                copy.wait_recv()
            place = places[name]((x + 2) % NX, c)
            far.append(swap(name, i + 7, place, place))

    def ready(name):
        if name in gathers:
            pass_on(name)
            pass_far(name)
            own[name].wait()
            for copy in gathers.pop(name)[1]:
                copy.wait_recv()

    flights, slots = {}, {}

    def send(name, s, moves):
        copies = []
        for src, dst, device in moves:
            i = slots[s] = slots.get(s, -1) + 1
            copies.append(remote(src, dst, ssem.at[s, i], rsem.at[s, i], device))
        flights[name, s] = copies

    def arrive(name, s):
        for copy in flights.pop((name, s), ()):
            copy.wait_recv()

    def part(s):
        return slice(s * T, (s + 1) * T)

    def low(at):
        return 2 * ((x // 2 + at) % 2) + at // 2

    def spread(s):
        landed(ctx_all.at[z, 0:T], csem.at[0])
        piece = ctx_all.at[z, part(0), :]
        send("spread", 0, [(piece, piece, zp(d)) for d in (4, 3, 5, 2, 6, 1, 7)])

    def ring(t):
        def step(g):
            members = GROUPS[g]
            span = slice(members[0] * T, (members[-1] + 1) * T)
            if t == 0:
                if g == 0:
                    landed(ctx_all.at[z, T:H], csem.at[1])
            else:
                arrive("ctx%d" % (t - 1), S + g)
            cols = (slice(0, K // 2), slice(K // 2, K)) if t == 3 else (slice(0, K), slice(0, K))
            up_piece, down_piece = ctx_all.at[zi(-t), span, cols[0]], ctx_all.at[zi(t), span, cols[1]]
            send("ctx%d" % t, S + g, [(up_piece, up_piece, zp(1)), (down_piece, down_piece, zp(-1))])
        return step

    def scatter(name, s, product, piece, landing):
        k = part(s)
        piece[:, :, k, :] = product.astype(jnp.bfloat16).reshape(2, 4, T, 2 * F)
        send(name, s, [(piece.at[:, low(yi(d)), k, :], landing.at[d - 1, :, k, :], yp(d)) for d in (1, 3, 2)])

    def scattered(name, s, piece, landing):
        arrive(name, s)
        k = part(s)
        total = piece[:, low(y), k, :].astype(jnp.float32)
        for d in range(3):
            total = total + landing[d, :, k, :].astype(jnp.float32)
        return total.reshape(2 * T, 2 * F)

    def project(s):
        if s == 0:
            pass_on("proj")
            gather("up", 1)
            arrive("spread", 0)
        else:
            arrive("ctx3", S + [s in members for members in GROUPS].index(True))
        ready("proj")
        product = jnp.dot(ctx_all[:, part(s), :].reshape(NZ * T, K), wproj[...], preferred_element_type=jnp.float32)
        scatter("project", s, product, att, rs)

    def mix(s):
        total = scattered("project", s, att, rs)
        k = part(s)
        if s == 0:
            landed(resb, csem.at[2])
            vec_swap[0].wait_recv()
        row_sum, row_square = jnp.zeros((2 * T, 128), jnp.float32), jnp.zeros((2 * T, 128), jnp.float32)
        for h in range(2):
            value = resb[h, :, k, :].reshape(2 * T, F).astype(jnp.float32) + total[:, h * F:(h + 1) * F] + vec[h, 0:1, :]
            mixed[h, s] = value
            for i in range(0, F, 128):
                row_sum = row_sum + value[:, i:i + 128]
                row_square = row_square + value[:, i:i + 128] * value[:, i:i + 128]
        pad = jnp.zeros((64 - 2 * T, 128), jnp.float32)
        by_lane = jnp.concatenate([row_sum, pad, row_square, pad], axis=0).T
        st[s, z] = jnp.sum(by_lane, axis=0, keepdims=True)
        send("mix", s, [(st.at[s, z], st.at[s, z], zp(d)) for d in (4, 3, 5, 2, 6, 1, 7)])

    def norm(s):
        arrive("mix", s)
        k = part(s)
        total = jnp.broadcast_to(jnp.sum(st[s], axis=0), (128, 128)).T
        mean = total[0:2 * T, 0:1] / D
        var = total[64:64 + 2 * T, 0:1] / D - mean * mean
        scale = lax.rsqrt(var + 1e-05)
        for h in range(2):
            normed = (mixed[h, s] - mean) * scale * vec[h, 1:2, :] + vec[h, 2:3, :]
            nrm[:, low(y), k, h * F:(h + 1) * F] = normed.astype(jnp.bfloat16).reshape(2, T, F)
        piece = nrm.at[:, low(y), k, :]
        send("norm", s, [(piece, piece, yp(d)) for d in (1, 3, 2)])
        if s == 0:
            pass_on("up")
            gather("down", 2)

    def up(s):
        arrive("norm", s)
        ready("up")
        k = part(s)
        product = jnp.dot(nrm[:, :, k, :].reshape(NZ * T, 2 * F), wup[...], preferred_element_type=jnp.float32)
        prep[:, k, :] = product.astype(jnp.bfloat16).reshape(NZ, T, U)
        send("up", s, [
            (prep.at[zi(4), k, 0:U // 2], zr.at[0, 0, k, 0:U // 2], zp(1)),
            (prep.at[zi(4), k, U // 2:U], zr.at[1, 0, k, U // 2:U], zp(-1)),
        ])

    def passing(t):
        def step(s):
            arrive("up" if t == 1 else "pass%d" % (t - 1), s)
            k, moves = part(s), []
            for way, sign in ((0, 1), (1, -1)):
                at = zi(sign * (4 - t))
                cols = slice(0, U) if t > 1 else slice(way * (U // 2), (way + 1) * (U // 2))
                prep[at, k, cols] = (
                    prep[at, k, cols].astype(jnp.float32) + zr[way, t - 1, k, cols].astype(jnp.float32)
                ).astype(jnp.bfloat16)
                moves.append((prep.at[at, k, :], zr.at[way, t, k, :], zp(sign)))
            send("pass%d" % t, s, moves)
        return step

    def gelu(s):
        arrive("pass3", s)
        if s == 0:
            for copy in uvec_gather:
                copy.wait_recv()
        k = part(s)
        for i in range(NX):
            cols = slice(i * 2 * F, (i + 1) * 2 * F)
            total = prep[z, k, cols].astype(jnp.float32) + zr[0, 3, k, cols].astype(jnp.float32)
            total = total + zr[1, 3, k, cols].astype(jnp.float32) + uvec[i, 0:1, :]
            hid[z, k, cols] = jax.nn.gelu(total, approximate=True).astype(jnp.bfloat16)
        piece = hid.at[z, k, :]
        send("gelu", s, [(piece, piece, zp(1)), (piece, piece, zp(-1))])

    def handing(t):
        def step(s):
            arrive("gelu" if t == 1 else "hand%d" % (t - 1), s)
            cols = (slice(0, U // 2), slice(U // 2, U)) if t == 3 else (slice(0, U), slice(0, U))
            up_piece, down_piece = hid.at[zi(-t), part(s), cols[0]], hid.at[zi(t), part(s), cols[1]]
            send("hand%d" % t, s, [(up_piece, up_piece, zp(1)), (down_piece, down_piece, zp(-1))])
            if t == 1 and s == 0:
                pass_on("down")
        return step

    def down(s):
        arrive("hand3", s)
        ready("down")
        product = jnp.dot(hid[:, part(s), :].reshape(NZ * T, U), wdown[...], preferred_element_type=jnp.float32)
        scatter("down", s, product, outp, os)

    def finish(s):
        total = scattered("down", s, outp, os)
        for h in range(2):
            value = mixed[h, s] + total[:, h * F:(h + 1) * F] + vec[h, 3:4, :]
            obuf[h, s] = value.astype(jnp.bfloat16)
        for h in range(2):
            for k in range(2):
                give(obuf.at[h, s, k * T:(k + 1) * T], out.at[rows(128 * c + 64 * (x % 2) + s * T, T)],
                     gsem.at[12 + s * 4 + h * 2 + k], csem.at[3], h, (x // 2 + y) % 2 + 2 * k)

    stages = dict(spread=spread, project=project, mix=mix, norm=norm, up=up, gelu=gelu, down=down, finish=finish)
    for t in range(1, 4):
        stages["pass%d" % t], stages["hand%d" % t] = passing(t), handing(t)
    for t in range(4):
        stages["ctx%d" % t] = ring(t)
    for name, index in issue_order()[0]:
        stages[name](index)
        clear(40)
    clear(0)
    landed(out, csem.at[3])


def layer(context, residual_in, proj_weight, proj_bias, norm_gain, norm_shift, up_weight, up_bias, down_weight, down_bias):
    bf16, f32 = jnp.bfloat16, jnp.float32
    hbm = pl.BlockSpec(memory_space=pl.ANY)
    dma = pltpu.SemaphoreType.DMA
    return pl.pallas_call(
        kernel,
        out_shape=jax.ShapeDtypeStruct((256, F), bf16),
        in_specs=[hbm] * 10,
        out_specs=hbm,
        scratch_shapes=[
            pltpu.VMEM((NZ, H, K), bf16),
            pltpu.VMEM((K, 2 * F), bf16),
            pltpu.VMEM((2 * F, U), bf16),
            pltpu.VMEM((U, 2 * F), bf16),
            pltpu.VMEM((2, 2, H, F), bf16),
            *[pltpu.VMEM((F,), bf16)] * 4,
            pltpu.VMEM((2 * F,), bf16),
            pltpu.VMEM((2, 8, F), f32),
            pltpu.VMEM((NX, 8, 2 * F), f32),
            pltpu.VMEM((2, 4, H, 2 * F), bf16),
            pltpu.VMEM((3, 2, H, 2 * F), bf16),
            pltpu.VMEM((2, S, 2 * T, F), f32),
            pltpu.VMEM((S, NZ, 1, 128), f32),
            pltpu.VMEM((2, 4, H, 2 * F), bf16),
            pltpu.VMEM((NZ, H, U), bf16),
            pltpu.VMEM((2, 4, H, U), bf16),
            pltpu.VMEM((NZ, H, U), bf16),
            pltpu.VMEM((2, 4, H, 2 * F), bf16),
            pltpu.VMEM((3, 2, H, 2 * F), bf16),
            pltpu.VMEM((2, S, 2 * T, F), bf16),
            dma((S + len(GROUPS), 44)),
            dma((S + len(GROUPS), 44)),
            dma((28,)),
            dma((28,)),
            dma((4,)),
            dma((12 + 4 * S,)),
            dma((8,)),
        ],
        compiler_params=pltpu.CompilerParams(
            collective_id=0, has_side_effects=True, vmem_limit_bytes=56 * 2**20
        ),
        name="layer",
    )(context, residual_in, proj_weight, proj_bias, norm_gain, norm_shift, up_weight, up_bias, down_weight, down_bias)


def solution(mesh):
    return jax.shard_map(
        layer,
        mesh=mesh,
        in_specs=(
            P("row", "col"),
            P("col", "row"),
            P("col", "row"),
            P("row"),
            P("row"),
            P("row"),
            P("row", "col"),
            P("col"),
            P("col", "row"),
            P("row"),
        ),
        out_specs=P("col", "row"),
        check_vma=False,
    )
```

time: 434 us -> 141 us (0.32)
  waiting for transfers between devices: 364 us -> 0 us
  Pallas kernels: 0 us -> 139 us
  blocking collectives: 25.7 us -> 0 us
  matrix products: 21.5 us -> 0 us
  between operations: 13.5 us -> 0.01 us
  other arithmetic: 6.65 us -> 0 us
    reduce_scatter x3 -> x0, waiting for transfers between devices: 216 us -> none  [the longest x1 76.8 us: local(): lax.psum_scatter(jnp.dot(rows_part, proj_weight, preferred_element_type=j...]
    all_gather x3 -> x0, waiting for transfers between devices: 147 us -> none  [the longest x1 51.6 us: local(): normed_all = lax.all_gather(normed, 'col', axis=0, tiled=True)]
    pallas_call x0 -> x1, Pallas kernels: none -> 139 us  [layer(): pl.pallas_call(kernel, out_shape=jax.ShapeDtypeStruct((256, F), bf16), in...]
    psum x1 -> x0, blocking collectives: 25.7 us -> none  [local(): lax.psum((jnp.sum(mixed, axis=1, keepdims=True), jnp.sum(mixed * mixed, a...]
    dot_general x3 -> x0, matrix products: 21.5 us -> none  [the longest x1 7.97 us: local(): jnp.dot(rows_part, up_weight, preferred_element_type=jnp.float32)]
    convert_element_type x8 -> x0, other arithmetic: 5.53 us -> none  [the longest x1 2.05 us: local(): jax.nn.gelu(pre_local + up_bias.astype(jnp.float32), approximate=True)]
  transfers between devices with their start and end apart: 6 -> 0, of which waited for: 6 -> 0; matrix products, arithmetic and copies ran while one was open for 0% -> 0% of each run, Pallas kernels for 0% -> 0%
where the time goes in v3:
time: 141 us
  Pallas kernels  139 us (99%)
  local copies, waits for them, and re-layouts  1.62 us (1%)
    pallas_call x1, Pallas kernels, layer(): pl.pallas_call(kernel, out_shape=jax.ShapeDtypeStruct((256, F), bf16), in...  139 us

profile of v3, /device:TPU:1, one launch (start us, length us, event | category | flops | bytes accessed | tf_op | source)
XLA Modules:
  0.0 140.8 jit_solution(12012868926397290147)
XLA Ops:
  0.0 139.2 %layer.1 = bf16[256,384]{1,0:T(8,128)(2,1)} custom-call(bf16[256,384]{1,0:T(8,128)(2,1)} %ctx.1, bf16[256,384]{1,0:T(8,128)(2,1)} %res.1, bf16[384,384]{1,0:T(8,128)(2,1)} %wp.1, bf16[384]{0:T(512)(128)(2,1)} %pb.1, bf16[384]{0:T(512)(128)(2,1)} %ng.1, bf16[384]{0:T(512)(128)(2,1)} %ns.1, bf16[384,768]{1,0:T(8,128)(2,1)} %wu.1, bf16[768]{0:T(1024)(128)(2,1)} %ub.1, ...), custom_call_target="tpu_custom_call" | custom-call | tf_op jit(solution)/shard_map/layer/pallas_call | solution.py:396
  139.2 1.6 %copy.12 = bf16[256,384]{1,0:T(8,128)(2,1)} copy(bf16[256,384]{1,0:T(8,128)(2,1)} %layer.1) | data formatting | bytes 393216

commit v4 on v3

--- a/solution.py
+++ b/solution.py
@@ -16,51 +16,59 @@
 NZ, NX, NY = 8, 4, 4
 MESH = pl.DeviceIdType.MESH
 
-CHAIN = (
-    ("project", 3, "y", 98304, 2.7, 0.6),
-    ("mix", 7, "z", 0, 4.3, 0.6),
-    ("norm", 3, "y", 98304, 2.7, 0.5),
-    ("up", 2, "z", 49152, 2.8, 0.9),
-    ("pass1", 2, "z", 98304, 2.8, 0.25),
-    ("pass2", 2, "z", 98304, 2.8, 0.25),
-    ("pass3", 2, "z", 98304, 2.8, 0.25),
-    ("gelu", 2, "z", 98304, 2.8, 0.5),
-    ("hand1", 2, "z", 98304, 2.8, 0.0),
-    ("hand2", 2, "z", 98304, 2.8, 0.0),
-    ("hand3", 2, "z", 49152, 2.8, 0.0),
-    ("down", 3, "y", 98304, 2.7, 0.9),
-    ("finish", 4, "x", 49152, 2.7, 0.4),
-)
+PARTS = (((0, 3 * U // 4), (3 * U // 4, U)),) + (((0, U),),) * (S - 1)
 RATE = 50000.0
-LOADED = {"project": 24.0, "up": 42.0, "down": 62.0}
+Z_STEPS = ("up", "pass1", "pass2", "pass3", "gelu", "hand1", "hand2", "hand3")
+Z_WORK = dict(up=0.9, pass1=0.25, pass2=0.25, pass3=0.25, gelu=0.5)
 
 
 def issue_order():
-    chains = [[("spread", 7, "z", 393216, 4.3, 0.0, 0)] + [st + (0,) for st in CHAIN]]
-    chains += [[st + (s,) for st in CHAIN] for s in range(1, S)]
+    nodes = {
+        ("relay_proj", 0, 0): ((), 16.5, 0.0, 4, "x", 0, 0.0),
+        ("share_proj", 0, 0): ((("relay_proj", 0, 0),), 20.0, 0.0, 2, "x", 0, 0.0),
+        ("relay_up", 0, 0): ((("share_proj", 0, 0),), 32.0, 0.0, 4, "x", 0, 0.0),
+        ("share_up", 0, 0): ((("relay_up", 0, 0),), 39.0, 0.0, 2, "x", 0, 0.0),
+        ("relay_down", 0, 0): ((("share_up", 0, 0),), 52.0, 0.0, 4, "x", 0, 0.0),
+        ("share_down", 0, 0): ((("relay_down", 0, 0),), 62.0, 0.0, 2, "x", 0, 0.0),
+        ("spread", 0, 0): ((), 14.0, 0.0, 7, "z", 393216, 4.3),
+    }
+    arrived = {0: ("spread", 0, 0)}
+    for s in range(S):
+        if s > 0:
+            g = [s in members for members in GROUPS].index(True)
+            arrived[s] = ("ctx3", g, 0)
+        nodes["project", s, 0] = ((arrived[s],), 25.0, 0.6, 3, "y", 98304, 2.7)
+        nodes["mix", s, 0] = ((("project", s, 0),), 0.0, 0.6, 7, "z", 0, 4.3)
+        nodes["norm", s, 0] = ((("mix", s, 0),), 0.0, 0.5, 3, "y", 98304, 2.7)
+        for u, (first_unit, last_unit) in enumerate(PARTS[s]):
+            share = (last_unit - first_unit) / U
+            before = ("norm", s, 0)
+            for name in Z_STEPS:
+                size = 98304 * share * (0.5 if name in ("up", "hand3") else 1)
+                nodes[name, s, u] = ((before,), 46.0 if (name, u) == ("up", 1) else 0.0, Z_WORK.get(name, 0.0) * share, 2, "z", size, 2.8)
+                before = (name, s, u)
+        nodes["down", s, 0] = (tuple(("hand3", s, u) for u in range(len(PARTS[s]))), 0.0, 0.9, 3, "y", 98304, 2.7)
+        nodes["finish", s, 0] = ((("down", s, 0),), 0.0, 0.4, 4, "x", 49152, 2.7)
     for g, members in enumerate(GROUPS):
-        chains.append([("ctx%d" % t, 2, "z", 49152 * len(members) * (0.5 if t == 3 else 1), 2.8, 0.0, g) for t in range(4)])
-    waits = {s: S + g for g, members in enumerate(GROUPS) for s in members}
-    place, ready = [0] * len(chains), [16.0] * len(chains)
-    for s in range(1, S):
-        ready[s] = float("inf")
-    free, now, order = {"z": 0.0, "y": 0.0, "x": 0.0}, 0.0, []
-    while any(p < len(ch) for p, ch in zip(place, chains)):
-        live = [i for i in range(len(chains)) if place[i] < len(chains[i])]
-        due_at = {i: max(ready[i], LOADED.get(chains[i][place[i]][0], 0.0)) for i in live}
-        first = min(due_at.values())
-        i = min(i for i in live if due_at[i] <= max(now, first))
-        name, copies, link, size, latency, work, index = chains[i][place[i]]
-        now = max(now, due_at[i]) + work + 0.08 * copies
+        for t in range(4):
+            size = 49152 * len(members) * (0.5 if t == 3 else 1)
+            nodes["ctx%d" % t, g, 0] = (((("ctx%d" % (t - 1), g, 0),) if t else ()), 20.5 if t == 0 else 0.0, 0.0, 2, "z", size, 2.8)
+    urgency = {node: (node[0].startswith("ctx"), node[1], node[2]) for node in nodes}
+    free, now, order, done = {"z": 0.0, "y": 0.0, "x": 0.0}, 0.0, [], {}
+    while len(order) < len(nodes):
+        due = {
+            node: max([start] + [done[n] for n in after])
+            for node, (after, start, *_) in nodes.items()
+            if node not in done and all(n in done for n in after)
+        }
+        first = min(due.values())
+        node = min((n for n in due if due[n] <= max(now, first)), key=lambda n: (urgency[n], n))
+        _, _, work, copies, link, size, latency = nodes[node]
+        now = max(now, due[node]) + work + 0.06 * copies
         free[link] = max(free[link], now) + size / RATE
-        ready[i] = free[link] + latency
-        place[i] += 1
-        order.append((name, index))
-        if i >= S and place[i] == len(chains[i]):
-            for s, chain in waits.items():
-                if chain == i:
-                    ready[s] = ready[i]
-    return order, max(ready[:S])
+        done[node] = free[link] + latency
+        order.append(node)
+    return order, max(done.values())
 
 
 def kernel(ctx, res, wp, pb, ng, ns, wu, ub, wd, db, out,
@@ -138,13 +146,13 @@
     vin = (vin0, vin1, vin2, vin3)
     half = lanes(c * F, F)
     places = {
-        "proj": lambda at, core: wproj.at[rows(at * F, F), lanes(core * F, F)],
-        "up": lambda at, core: wup.at[rows(core * F, F), lanes(at * 2 * F, 2 * F)],
-        "down": lambda at, core: wdown.at[rows(at * 2 * F, 2 * F), lanes(core * F, F)],
+        "proj": lambda slot: wproj.at[slot * F:(slot + 1) * F, half],
+        "up": lambda slot: wup.at[rows(c * F, F), slot * 2 * F:(slot + 1) * 2 * F],
+        "down": lambda slot: wdown.at[slot * 2 * F:(slot + 1) * 2 * F, half],
     }
     blocks = {"proj": wp, "up": wu, "down": wd}
     vector_in = [local(v, vin[i], lsem.at[i]) for i, v in enumerate((pb, ng, ns, db))] + [local(ub, uin, lsem.at[4])]
-    own = {name: local(blocks[name], places[name](x, c), lsem.at[5 + i]) for i, name in enumerate(blocks)}
+    own = {name: local(blocks[name], places[name](0), lsem.at[5 + i]) for i, name in enumerate(blocks)}
 
     barrier = pltpu.get_barrier_semaphore()
     partners = [sib] + [zp(d) for d in range(1, NZ)] + [yp(d) for d in range(1, NY)]
@@ -153,68 +161,77 @@
         pl.semaphore_signal(barrier, inc=1, device_id=p, device_id_type=MESH)
     pl.semaphore_wait(barrier, len(partners))
 
+    gathers = {}
+
+    def swap(name, i, src, dst):
+        return remote(src, dst, wssem.at[i], wrsem.at[i], sib)
+
+    def halves(place):
+        n = place.shape[0] // 2
+        return place.at[0:n], place.at[n:2 * n]
+
+    def gather(name, i):
+        block, near = halves(blocks[name]), {}
+        for first in (True, False):
+            for j, d in ((0, 1), (1, 3)):
+                k = j if first else 1 - j
+                n = i + 2 * j + (0 if first else 1)
+                near[j, first] = remote(block[k], halves(places[name](1 + j))[k], wssem.at[n], wrsem.at[n], xp(d))
+        gathers[name] = (near, [swap(name, i + 4, blocks[name], places[name](0))], [], i)
+
     ctx_side = (c + z // 2) % 2
-    for g, (low, size) in enumerate(((0, T), (T, H - T))):
+
+    def slot_at(at):
+        d = (x - at + NX) % NX
+        return jnp.where(d == 3, 1, jnp.where(d == 0, 0, d + 1))
+
+    def give_context(g, low, size):
         for i in range(2):
             for core in range(2):
-                give(ctx.at[rows(128 * core + 64 * i + low, size)], ctx_all.at[z, low:low + size, lanes(x * F, F)],
+                give(ctx.at[rows(128 * core + 64 * i + low, size)], ctx_all.at[z, low:low + size, lanes(slot_at(2 * ctx_side + i) * F, F)],
                      gsem.at[g * 4 + i * 2 + core], csem.at[g], core, 2 * ctx_side + i)
-    gathers = {}
-
-    def swap(name, i, src, dst):
-        return remote(src, dst, wssem.at[i], wrsem.at[i], sib)
-
-    def gather(name, i):
-        mine = places[name](x, c)
-        gathers[name] = (
-            [remote(blocks[name], mine, wssem.at[8 * i + d], wrsem.at[8 * i + d], xp(d)) for d in (1, 3)],
-            [swap(name, 8 * i, blocks[name], mine)],
-            [],
-            8 * i,
-        )
-
+
+    def give_residual():
+        side = (x + y) % 2
+        for i in range(2):
+            for core in range(2):
+                give(res.at[rows(128 * core + 64 * i, H)], resb.at[c, x // 2], gsem.at[8 + i * 2 + core], csem.at[2],
+                     core, 2 * side + i)
+
+    give_context(0, 0, T)
     gather("proj", 0)
-    side = (x + y) % 2
-    for i in range(2):
-        for core in range(2):
-            give(res.at[rows(128 * core + 64 * i, H)], resb.at[c, x // 2], gsem.at[8 + i * 2 + core], csem.at[2], core, 2 * side + i)
+    give_context(1, T, H - T)
     for copy in vector_in:
         copy.wait()
     for i in range(4):
         vec[c, i:i + 1, :] = vin[i][...].reshape(1, F).astype(jnp.float32)
-    uvec[x, 0:1, :] = uin[...].reshape(1, 2 * F).astype(jnp.float32)
-    vec_swap = [swap("vec", 24, vec.at[c], vec.at[c])]
-    uvec_gather = [remote(uvec.at[x], uvec.at[x], wssem.at[24 + d], wrsem.at[24 + d], xp(d)) for d in (1, 3, 2)]
-
-    def pass_on(name):
+    uvec[0, 0:1, :] = uin[...].reshape(1, 2 * F).astype(jnp.float32)
+    vec_swap = [swap("vec", 30, vec.at[c], vec.at[c])]
+    uvec_gather = [remote(uvec.at[0], uvec.at[{1: 1, 3: 2, 2: 3}[d]], wssem.at[30 + d], wrsem.at[30 + d], xp(d)) for d in (1, 3, 2)]
+
+    def relay(name):
         near, far, relays, i = gathers[name]
-        if not relays:
-            for copy in near:
+        for j, to in ((0, 1), (1, 3)):
+            near[j, True].wait_recv()
+            piece, goal = halves(places[name](1 + j))[j], halves(places[name](3))[j]
+            relays.append(remote(piece, goal, wssem.at[i + 5 + j], wrsem.at[i + 5 + j], xp(to)))
+
+    def share(name):
+        near, far, relays, i = gathers[name]
+        for j in range(2):
+            near[j, False].wait_recv()
+            far.append(swap(name, i + 7 + j, places[name](1 + j), places[name](1 + j)))
+
+    def ready(name, near_only=False):
+        if name in own:
+            own.pop(name).wait()
+            for copy in gathers[name][1]:
                 copy.wait_recv()
-            for j, (d, to) in enumerate(((-1, 1), (1, 3))):
-                place = places[name]((x + d + NX) % NX, c)
-                n = place.shape[0] // 2
-                piece = place.at[j * n:(j + 1) * n]
-                relays.append(remote(piece, piece, wssem.at[i + 4 + j], wrsem.at[i + 4 + j], xp(to)))
-            for j, d in enumerate((-1, 1)):
-                place = places[name]((x + d + NX) % NX, c)
-                far.append(swap(name, i + (2, 6)[j], place, place))
-
-    def pass_far(name):
-        near, far, relays, i = gathers[name]
-        if len(far) == 3:
+        if name in gathers and not near_only:
+            near, far, relays, i = gathers.pop(name)
             for copy in relays:
                 copy.wait_recv()
-            place = places[name]((x + 2) % NX, c)
-            far.append(swap(name, i + 7, place, place))
-
-    def ready(name):
-        if name in gathers:
-            pass_on(name)
-            pass_far(name)
-            own[name].wait()
-            for copy in gathers.pop(name)[1]:
-                copy.wait_recv()
+            swap(name, i + 9, places[name](3), places[name](3)).wait_recv()
 
     flights, slots = {}, {}
 
@@ -269,8 +286,6 @@
 
     def project(s):
         if s == 0:
-            pass_on("proj")
-            gather("up", 1)
             arrive("spread", 0)
         else:
             arrive("ctx3", S + [s in members for members in GROUPS].index(True))
@@ -308,61 +323,66 @@
             nrm[:, low(y), k, h * F:(h + 1) * F] = normed.astype(jnp.bfloat16).reshape(2, T, F)
         piece = nrm.at[:, low(y), k, :]
         send("norm", s, [(piece, piece, yp(d)) for d in (1, 3, 2)])
-        if s == 0:
-            pass_on("up")
-            gather("down", 2)
-
-    def up(s):
-        arrive("norm", s)
-        ready("up")
-        k = part(s)
-        product = jnp.dot(nrm[:, :, k, :].reshape(NZ * T, 2 * F), wup[...], preferred_element_type=jnp.float32)
-        prep[:, k, :] = product.astype(jnp.bfloat16).reshape(NZ, T, U)
-        send("up", s, [
-            (prep.at[zi(4), k, 0:U // 2], zr.at[0, 0, k, 0:U // 2], zp(1)),
-            (prep.at[zi(4), k, U // 2:U], zr.at[1, 0, k, U // 2:U], zp(-1)),
+
+
+    def columns(s, u):
+        start, stop = PARTS[s][u]
+        middle = (start + stop) // 2
+        return slice(start, stop), (slice(start, middle), slice(middle, stop))
+
+    def up(s, u):
+        if u == 0:
+            arrive("norm", s)
+        ready("up", (s, u) == (0, 0))
+        k, (cols, sides) = part(s), columns(s, u)
+        product = jnp.dot(nrm[:, :, k, :].reshape(NZ * T, 2 * F), wup[:, cols], preferred_element_type=jnp.float32)
+        prep[:, k, cols] = product.astype(jnp.bfloat16).reshape(NZ, T, cols.stop - cols.start)
+        send(("up", u), s, [
+            (prep.at[zi(4), k, sides[0]], zr.at[0, 0, k, sides[0]], zp(1)),
+            (prep.at[zi(4), k, sides[1]], zr.at[1, 0, k, sides[1]], zp(-1)),
         ])
 
     def passing(t):
-        def step(s):
-            arrive("up" if t == 1 else "pass%d" % (t - 1), s)
-            k, moves = part(s), []
+        def step(s, u):
+            arrive(("up" if t == 1 else "pass%d" % (t - 1), u), s)
+            k, (cols, sides), moves = part(s), columns(s, u), []
             for way, sign in ((0, 1), (1, -1)):
                 at = zi(sign * (4 - t))
-                cols = slice(0, U) if t > 1 else slice(way * (U // 2), (way + 1) * (U // 2))
-                prep[at, k, cols] = (
-                    prep[at, k, cols].astype(jnp.float32) + zr[way, t - 1, k, cols].astype(jnp.float32)
+                came = cols if t > 1 else sides[way]
+                prep[at, k, came] = (
+                    prep[at, k, came].astype(jnp.float32) + zr[way, t - 1, k, came].astype(jnp.float32)
                 ).astype(jnp.bfloat16)
-                moves.append((prep.at[at, k, :], zr.at[way, t, k, :], zp(sign)))
-            send("pass%d" % t, s, moves)
+                moves.append((prep.at[at, k, cols], zr.at[way, t, k, cols], zp(sign)))
+            send(("pass%d" % t, u), s, moves)
         return step
 
-    def gelu(s):
-        arrive("pass3", s)
-        if s == 0:
+    def gelu(s, u):
+        arrive(("pass3", u), s)
+        if (s, u) == (0, 0):
             for copy in uvec_gather:
                 copy.wait_recv()
-        k = part(s)
-        for i in range(NX):
-            cols = slice(i * 2 * F, (i + 1) * 2 * F)
-            total = prep[z, k, cols].astype(jnp.float32) + zr[0, 3, k, cols].astype(jnp.float32)
-            total = total + zr[1, 3, k, cols].astype(jnp.float32) + uvec[i, 0:1, :]
-            hid[z, k, cols] = jax.nn.gelu(total, approximate=True).astype(jnp.bfloat16)
-        piece = hid.at[z, k, :]
-        send("gelu", s, [(piece, piece, zp(1)), (piece, piece, zp(-1))])
+        k, (cols, _) = part(s), columns(s, u)
+        for i in range(cols.start, cols.stop, F):
+            at = slice(i, i + F)
+            total = prep[z, k, at].astype(jnp.float32) + zr[0, 3, k, at].astype(jnp.float32)
+            unit = i % (2 * F)
+            total = total + zr[1, 3, k, at].astype(jnp.float32) + uvec[i // (2 * F), 0:1, unit:unit + F]
+            hid[z, k, at] = jax.nn.gelu(total, approximate=True).astype(jnp.bfloat16)
+        piece = hid.at[z, k, cols]
+        send(("gelu", u), s, [(piece, piece, zp(1)), (piece, piece, zp(-1))])
 
     def handing(t):
-        def step(s):
-            arrive("gelu" if t == 1 else "hand%d" % (t - 1), s)
-            cols = (slice(0, U // 2), slice(U // 2, U)) if t == 3 else (slice(0, U), slice(0, U))
-            up_piece, down_piece = hid.at[zi(-t), part(s), cols[0]], hid.at[zi(t), part(s), cols[1]]
-            send("hand%d" % t, s, [(up_piece, up_piece, zp(1)), (down_piece, down_piece, zp(-1))])
-            if t == 1 and s == 0:
-                pass_on("down")
+        def step(s, u):
+            arrive(("gelu" if t == 1 else "hand%d" % (t - 1), u), s)
+            cols, sides = columns(s, u)
+            ways = sides if t == 3 else (cols, cols)
+            up_piece, down_piece = hid.at[zi(-t), part(s), ways[0]], hid.at[zi(t), part(s), ways[1]]
+            send(("hand%d" % t, u), s, [(up_piece, up_piece, zp(1)), (down_piece, down_piece, zp(-1))])
         return step
 
     def down(s):
-        arrive("hand3", s)
+        for u in range(len(PARTS[s])):
+            arrive(("hand3", u), s)
         ready("down")
         product = jnp.dot(hid[:, part(s), :].reshape(NZ * T, U), wdown[...], preferred_element_type=jnp.float32)
         scatter("down", s, product, outp, os)
@@ -377,14 +397,30 @@
                 give(obuf.at[h, s, k * T:(k + 1) * T], out.at[rows(128 * c + 64 * (x % 2) + s * T, T)],
                      gsem.at[12 + s * 4 + h * 2 + k], csem.at[3], h, (x // 2 + y) % 2 + 2 * k)
 
-    stages = dict(spread=spread, project=project, mix=mix, norm=norm, up=up, gelu=gelu, down=down, finish=finish)
-    for t in range(1, 4):
-        stages["pass%d" % t], stages["hand%d" % t] = passing(t), handing(t)
+    stages = {("spread", "project", "mix", "norm", "down", "finish")[i]: f
+              for i, f in enumerate((spread, project, mix, norm, down, finish))}
     for t in range(4):
         stages["ctx%d" % t] = ring(t)
-    for name, index in issue_order()[0]:
-        stages[name](index)
-        clear(40)
+    by_part = dict(up=up, gelu=gelu)
+    for t in range(1, 4):
+        by_part["pass%d" % t], by_part["hand%d" % t] = passing(t), handing(t)
+    for name, s, u in issue_order()[0]:
+        if name in by_part:
+            by_part[name](s, u)
+        elif name == "relay_proj":
+            relay("proj")
+            give_residual()
+            gather("up", 10)
+        elif name == "relay_up":
+            relay("up")
+            gather("down", 20)
+        elif name == "relay_down":
+            relay("down")
+        elif name.startswith("share_"):
+            share(name[6:])
+        else:
+            stages[name](s)
+        clear(60)
     clear(0)
     landed(out, csem.at[3])
 
@@ -419,10 +455,10 @@
             pltpu.VMEM((2, 4, H, 2 * F), bf16),
             pltpu.VMEM((3, 2, H, 2 * F), bf16),
             pltpu.VMEM((2, S, 2 * T, F), bf16),
-            dma((S + len(GROUPS), 44)),
-            dma((S + len(GROUPS), 44)),
-            dma((28,)),
-            dma((28,)),
+            dma((S + len(GROUPS), 56)),
+            dma((S + len(GROUPS), 56)),
+            dma((34,)),
+            dma((34,)),
             dma((4,)),
             dma((12 + 4 * S,)),
             dma((8,)),

time: 141 us -> 135 us (0.957)
  Pallas kernels: 139 us -> 134 us
    pallas_call x1, Pallas kernels: 139 us -> 134 us  [layer(): pl.pallas_call(kernel, out_shape=jax.ShapeDtypeStruct((256, F), bf16), in...]
where the time goes in v4:
time: 135 us
  Pallas kernels  134 us (99%)
  local copies, waits for them, and re-layouts  1.62 us (1%)
    pallas_call x1, Pallas kernels, layer(): pl.pallas_call(kernel, out_shape=jax.ShapeDtypeStruct((256, F), bf16), in...  134 us

profile of v4, /device:TPU:1, one launch (start us, length us, event | category | flops | bytes accessed | tf_op | source)
XLA Modules:
  0.0 135.2 jit_solution(13111347978647959214)
XLA Ops:
  0.0 133.5 %layer.1 = bf16[256,384]{1,0:T(8,128)(2,1)} custom-call(bf16[256,384]{1,0:T(8,128)(2,1)} %ctx.1, bf16[256,384]{1,0:T(8,128)(2,1)} %res.1, bf16[384,384]{1,0:T(8,128)(2,1)} %wp.1, bf16[384]{0:T(512)(128)(2,1)} %pb.1, bf16[384]{0:T(512)(128)(2,1)} %ng.1, bf16[384]{0:T(512)(128)(2,1)} %ns.1, bf16[384,768]{1,0:T(8,128)(2,1)} %wu.1, bf16[768]{0:T(1024)(128)(2,1)} %ub.1, ...), custom_call_target="tpu_custom_call" | custom-call | tf_op jit(solution)/shard_map/layer/pallas_call | solution.py:432
  133.5 1.6 %copy.12 = bf16[256,384]{1,0:T(8,128)(2,1)} copy(bf16[256,384]{1,0:T(8,128)(2,1)} %layer.1) | data formatting | bytes 393216

commit v5 on v4

--- a/solution.py
+++ b/solution.py
@@ -26,10 +26,10 @@
     nodes = {
         ("relay_proj", 0, 0): ((), 16.5, 0.0, 4, "x", 0, 0.0),
         ("share_proj", 0, 0): ((("relay_proj", 0, 0),), 20.0, 0.0, 2, "x", 0, 0.0),
-        ("relay_up", 0, 0): ((("share_proj", 0, 0),), 32.0, 0.0, 4, "x", 0, 0.0),
-        ("share_up", 0, 0): ((("relay_up", 0, 0),), 39.0, 0.0, 2, "x", 0, 0.0),
-        ("relay_down", 0, 0): ((("share_up", 0, 0),), 52.0, 0.0, 4, "x", 0, 0.0),
-        ("share_down", 0, 0): ((("relay_down", 0, 0),), 62.0, 0.0, 2, "x", 0, 0.0),
+        ("relay_up", 0, 0): ((("share_proj", 0, 0),), 34.5, 0.0, 4, "x", 0, 0.0),
+        ("share_up", 0, 0): ((("relay_up", 0, 0),), 41.0, 0.0, 2, "x", 0, 0.0),
+        ("relay_down", 0, 0): ((("share_up", 0, 0),), 62.0, 0.0, 4, "x", 0, 0.0),
+        ("share_down", 0, 0): ((("relay_down", 0, 0),), 75.0, 0.0, 2, "x", 0, 0.0),
         ("spread", 0, 0): ((), 14.0, 0.0, 7, "z", 393216, 4.3),
     }
     arrived = {0: ("spread", 0, 0)}
@@ -45,7 +45,7 @@
             before = ("norm", s, 0)
             for name in Z_STEPS:
                 size = 98304 * share * (0.5 if name in ("up", "hand3") else 1)
-                nodes[name, s, u] = ((before,), 46.0 if (name, u) == ("up", 1) else 0.0, Z_WORK.get(name, 0.0) * share, 2, "z", size, 2.8)
+                nodes[name, s, u] = ((before,), 50.0 if (name, u) == ("up", 1) else 0.0, Z_WORK.get(name, 0.0) * share, 2, "z", size, 2.8)
                 before = (name, s, u)
         nodes["down", s, 0] = (tuple(("hand3", s, u) for u in range(len(PARTS[s]))), 0.0, 0.9, 3, "y", 98304, 2.7)
         nodes["finish", s, 0] = ((("down", s, 0),), 0.0, 0.4, 4, "x", 49152, 2.7)
@@ -413,11 +413,12 @@
             gather("up", 10)
         elif name == "relay_up":
             relay("up")
-            gather("down", 20)
         elif name == "relay_down":
             relay("down")
         elif name.startswith("share_"):
             share(name[6:])
+            if name == "share_up":
+                gather("down", 20)
         else:
             stages[name](s)
         clear(60)

time: 135 us -> 135 us (level)
  no operation moved by 1% of the time
where the time goes in v5:
time: 135 us; the launch traced here: 134 us
  Pallas kernels  133 us (99%)
  local copies, waits for them, and re-layouts  1.62 us (1%)
    pallas_call x1, Pallas kernels, layer(): pl.pallas_call(kernel, out_shape=jax.ShapeDtypeStruct((256, F), bf16), in...  133 us

profile of v5, /device:TPU:1, one launch (start us, length us, event | category | flops | bytes accessed | tf_op | source)
XLA Modules:
  0.0 134.5 jit_solution(4788795074629305602)
XLA Ops:
  0.0 132.8 %layer.1 = bf16[256,384]{1,0:T(8,128)(2,1)} custom-call(bf16[256,384]{1,0:T(8,128)(2,1)} %ctx.1, bf16[256,384]{1,0:T(8,128)(2,1)} %res.1, bf16[384,384]{1,0:T(8,128)(2,1)} %wp.1, bf16[384]{0:T(512)(128)(2,1)} %pb.1, bf16[384]{0:T(512)(128)(2,1)} %ng.1, bf16[384]{0:T(512)(128)(2,1)} %ns.1, bf16[384,768]{1,0:T(8,128)(2,1)} %wu.1, bf16[768]{0:T(1024)(128)(2,1)} %ub.1, ...), custom_call_target="tpu_custom_call" | custom-call | tf_op jit(solution)/shard_map/layer/pallas_call | solution.py:433
  132.8 1.6 %copy.12 = bf16[256,384]{1,0:T(8,128)(2,1)} copy(bf16[256,384]{1,0:T(8,128)(2,1)} %layer.1) | data formatting | bytes 393216

commit v6 on v5

--- a/solution.py
+++ b/solution.py
@@ -16,7 +16,7 @@
 NZ, NX, NY = 8, 4, 4
 MESH = pl.DeviceIdType.MESH
 
-PARTS = (((0, 3 * U // 4), (3 * U // 4, U)),) + (((0, U),),) * (S - 1)
+PARTS = (((0, 3 * U // 4), (3 * U // 4, U)),) * 2 + (((0, U),),) * (S - 2)
 RATE = 50000.0
 Z_STEPS = ("up", "pass1", "pass2", "pass3", "gelu", "hand1", "hand2", "hand3")
 Z_WORK = dict(up=0.9, pass1=0.25, pass2=0.25, pass3=0.25, gelu=0.5)
@@ -45,7 +45,7 @@
             before = ("norm", s, 0)
             for name in Z_STEPS:
                 size = 98304 * share * (0.5 if name in ("up", "hand3") else 1)
-                nodes[name, s, u] = ((before,), 50.0 if (name, u) == ("up", 1) else 0.0, Z_WORK.get(name, 0.0) * share, 2, "z", size, 2.8)
+                nodes[name, s, u] = ((before,), 54.0 if name == "up" and u == len(PARTS[s]) - 1 else 0.0, Z_WORK.get(name, 0.0) * share, 2, "z", size, 2.8)
                 before = (name, s, u)
         nodes["down", s, 0] = (tuple(("hand3", s, u) for u in range(len(PARTS[s]))), 0.0, 0.9, 3, "y", 98304, 2.7)
         nodes["finish", s, 0] = ((("down", s, 0),), 0.0, 0.4, 4, "x", 49152, 2.7)
@@ -333,7 +333,7 @@
     def up(s, u):
         if u == 0:
             arrive("norm", s)
-        ready("up", (s, u) == (0, 0))
+        ready("up", u < len(PARTS[s]) - 1)
         k, (cols, sides) = part(s), columns(s, u)
         product = jnp.dot(nrm[:, :, k, :].reshape(NZ * T, 2 * F), wup[:, cols], preferred_element_type=jnp.float32)
         prep[:, k, cols] = product.astype(jnp.bfloat16).reshape(NZ, T, cols.stop - cols.start)

time: 135 us -> 134 us (level)
  no operation moved by 1% of the time
where the time goes in v6:
time: 134 us
  Pallas kernels  132 us (99%)
  local copies, waits for them, and re-layouts  1.62 us (1%)
    pallas_call x1, Pallas kernels, layer(): pl.pallas_call(kernel, out_shape=jax.ShapeDtypeStruct((256, F), bf16), in...  132 us

profile of v6, /device:TPU:1, one launch (start us, length us, event | category | flops | bytes accessed | tf_op | source)
XLA Modules:
  0.0 134.0 jit_solution(13580492454910431180)
XLA Ops:
  0.0 132.4 %layer.1 = bf16[256,384]{1,0:T(8,128)(2,1)} custom-call(bf16[256,384]{1,0:T(8,128)(2,1)} %ctx.1, bf16[256,384]{1,0:T(8,128)(2,1)} %res.1, bf16[384,384]{1,0:T(8,128)(2,1)} %wp.1, bf16[384]{0:T(512)(128)(2,1)} %pb.1, bf16[384]{0:T(512)(128)(2,1)} %ng.1, bf16[384]{0:T(512)(128)(2,1)} %ns.1, bf16[384,768]{1,0:T(8,128)(2,1)} %wu.1, bf16[768]{0:T(1024)(128)(2,1)} %ub.1, ...), custom_call_target="tpu_custom_call" | custom-call | tf_op jit(solution)/shard_map/layer/pallas_call | solution.py:433
  132.4 1.6 %copy.12 = bf16[256,384]{1,0:T(8,128)(2,1)} copy(bf16[256,384]{1,0:T(8,128)(2,1)} %layer.1) | data formatting | bytes 393216
